TPU v7x, 32 devices: a whole 2x2x4 slice. The times are simulated.
32 devices in a mesh: fsdp: 8 (over z, y), rep: 4 (over x, core).
Axes of the slice: x: 2, y: 2, z: 4, core: 2. Of those that a mesh axis runs over, the one named last changes fastest.
Arguments:
- tokens: bfloat16 [8192, 2048], P(('fsdp', 'rep')), may hold values from -6 to 6
- lengths: int32 [32], P(('fsdp', 'rep')), may hold values from 1 to 256, 5120 in all
- mixer_gain: bfloat16 [2048], P('fsdp'), may hold values from 0.5 to 1.5
- in_proj: bfloat16 [2048, 6704], P('fsdp'), may hold values from -0.125 to 0.125
- conv_weight: bfloat16 [4, 3584], P(None, 'fsdp'), may hold values from -3 to 3
- conv_bias: bfloat16 [3584], P('fsdp'), may hold values from -3 to 3
- decay_log: float32 [48], replicated, may hold values from 0 to 2.8
- step_bias: float32 [48], replicated, may hold values from -5 to -1
- skip_gain: float32 [48], replicated, may hold values from 0.5 to 1.5
- query_weight: bfloat16 [2048, 1024], P('fsdp'), may hold values from -0.125 to 0.125
- key_weight: bfloat16 [2048, 256], P('fsdp'), may hold values from -0.125 to 0.125
- value_weight: bfloat16 [2048, 256], P('fsdp'), may hold values from -0.125 to 0.125
- mamba_out: bfloat16 [3072, 2048], P('fsdp'), may hold values from -0.109375 to 0.109375
- attn_out: bfloat16 [1024, 2048], P('fsdp'), may hold values from -1 to 1
- mlp_gain: bfloat16 [2048], P('fsdp'), may hold values from 0.5 to 1.5
- gate_weight: bfloat16 [2048, 4096], P('fsdp'), may hold values from -0.125 to 0.125
- up_weight: bfloat16 [2048, 4096], P('fsdp'), may hold values from -0.125 to 0.125
- down_weight: bfloat16 [4096, 2048], P('fsdp'), may hold values from -0.09375 to 0.09375
- cotangent: bfloat16 [8192, 2048], P(('fsdp', 'rep')), may hold values from -6 to 6
Outputs:
- output: bfloat16 [8192, 2048], P(('fsdp', 'rep'))
- grad_tokens: bfloat16 [8192, 2048], P(('fsdp', 'rep'))
- grad_mixer_gain: float32 [2048], P('fsdp')
- grad_in_proj: float32 [2048, 6704], P('fsdp')
- grad_conv_weight: float32 [4, 3584], P(None, 'fsdp')
- grad_conv_bias: float32 [3584], P('fsdp')
- grad_decay_log: float32 [48], replicated
- grad_step_bias: float32 [48], replicated
- grad_skip_gain: float32 [48], replicated
- grad_query: float32 [2048, 1024], P('fsdp')
- grad_key: float32 [2048, 256], P('fsdp')
- grad_value: float32 [2048, 256], P('fsdp')
- grad_mamba_out: float32 [3072, 2048], P('fsdp')
- grad_attn_out: float32 [1024, 2048], P('fsdp')
- grad_mlp_gain: float32 [2048], P('fsdp')
- grad_gate: float32 [2048, 4096], P('fsdp')
- grad_up: float32 [2048, 4096], P('fsdp')
- grad_down: float32 [4096, 2048], P('fsdp')
Inputs may be any that keep to these rules, and one draw needn't show every extreme that they name: `lengths`: live length of each sequence; positions at or past it are padding. Some sequence is full in every draw.
All inputs are finite; a program needn't handle non-finite values. No bound on the sum of `lengths` on one device may be relied on, other than what follows from the above.
Results may differ from a plain program's by a relative error of at most 0.018.
Values may be sent and summed in bfloat16 or wider, within the bound.
A program may use at most 448 MiB of HBM per device.

v0:
```python
import jax
import jax.numpy as jnp
from jax import lax
from jax.sharding import PartitionSpec as P

HEADS = 48
HDIM = 64
STATE = 256
CONV = 4
QH = 8
KVH = 2
HEAD_WIDTH = 128
BLK = 128


epsilon = 1e-05


def rounding_rule():

    def rounded_value(values):
        return lax.optimization_barrier(values.astype(jnp.bfloat16)).astype(jnp.float32)

    def rounded_keep(values):
        return (rounded_value(values), None)

    def rounded_pass(stored, gradient):
        return (gradient,)

    wrapped = jax.custom_vjp(rounded_value)
    wrapped.defvjp(rounded_keep, rounded_pass)
    return wrapped


def passing_rule():

    def passed_value(values):
        return values

    def passed_keep(values):
        return (values, None)

    def passed_round(stored, gradient):
        return (low(gradient),)

    wrapped = jax.custom_vjp(passed_value)
    wrapped.defvjp(passed_keep, passed_round)
    return wrapped


def low(values):
    return rounding_rule()(values)


def low_back(values):
    return passing_rule()(values)


def forward_product(left, right):
    return jnp.dot(left, right, preferred_element_type=jnp.float32)


def left_product(left, right):
    return lax.dot_general(
        left, right, (((0,), (0,)), ((), ())), preferred_element_type=jnp.float32
    )


def right_product(left, right):
    return lax.dot_general(
        left, right, (((1,), (1,)), ((), ())), preferred_element_type=jnp.float32
    )


def rms_norm(values, gain):
    return values * lax.rsqrt(jnp.mean(values * values, axis=-1, keepdims=True) + epsilon) * gain


def norm_low(values, gain):
    return low(rms_norm(values, gain))


def gated_unit(gate_value, up_value):
    return low(jax.nn.silu(gate_value) * up_value)


def rotate(values):
    length = values.shape[0]
    half_width = values.shape[-1] // 2
    position = jnp.arange(length).astype(jnp.float32)
    freqs = 10000.0 ** (-jnp.arange(half_width).astype(jnp.float32) * 2.0 / values.shape[-1])
    angles = position[:, None] * freqs[None, :]
    cosine = jnp.cos(angles)[:, None, :]
    sine_part = jnp.sin(angles)[:, None, :]
    first_half = values[..., :half_width]
    second_half = values[..., half_width:]
    return jnp.concatenate(
        [
            first_half * cosine - second_half * sine_part,
            first_half * sine_part + second_half * cosine,
        ],
        axis=-1,
    )


def attention_core(query_proj, key_proj, value_proj):
    length = query_proj.shape[0]
    group_size = QH // KVH
    query_rot = low(rotate(query_proj.reshape(length, QH, HEAD_WIDTH)))
    rotated_key = low(rotate(key_proj.reshape(length, KVH, HEAD_WIDTH)))
    value_reduced = low(value_proj.reshape(length, KVH, HEAD_WIDTH))
    block_rows = min(length, 512)
    block_count = length // block_rows
    query_split = query_rot.reshape(block_count, block_rows, KVH, group_size, HEAD_WIDTH)
    starts = (jnp.arange(block_count) * block_rows).astype(jnp.int32)

    def attention_one_block(inputs):
        query_block_rows, start = inputs
        unscaled_value = jnp.einsum(
            "aklh,pkh->klap", query_block_rows, rotated_key, precision=lax.Precision.HIGHEST
        ) * HEAD_WIDTH ** (-0.5)
        scores = low_back(unscaled_value)
        index_of_row = start + jnp.arange(block_rows).astype(jnp.int32)
        col_index = jnp.arange(length).astype(jnp.int32)
        allowed = index_of_row[:, None] >= col_index[None, :]
        masked = jnp.where(allowed, scores, -1e30)
        probability_reduced = low(jax.nn.softmax(masked, axis=-1))
        return jnp.einsum(
            "kmou,ukf->okmf", probability_reduced, value_reduced, precision=lax.Precision.HIGHEST
        )

    result = lax.map(jax.checkpoint(attention_one_block), (query_split, starts))
    return result.reshape(length, QH * HEAD_WIDTH)


def ssd_scan(ssm_input, step_size, decay, input_map, output_map):
    length = ssm_input.shape[0]
    block_count = length // BLK
    blocks = (
        ssm_input.reshape(block_count, BLK, HEADS, HDIM),
        step_size.reshape(block_count, BLK, HEADS),
        decay.reshape(block_count, BLK, HEADS),
        input_map.reshape(block_count, BLK, STATE),
        output_map.reshape(block_count, BLK, STATE),
    )

    def ssd_one_block(ssm_state, inputs):
        block_input, block_step, block_decay, block_in_map, block_out_map = inputs
        running = jnp.cumsum(block_decay, axis=0)
        index_of_row = jnp.arange(BLK)
        lower_mask = (index_of_row[:, None] >= index_of_row[None, :])[:, :, None]
        decay_gap = running[:, None, :] - running[None, :, :]
        weight = jnp.where(lower_mask, jnp.exp(jnp.where(lower_mask, decay_gap, 0.0)), 0.0)
        pairing = jnp.dot(block_out_map, block_in_map.T, precision=lax.Precision.HIGHEST)
        mixing = pairing[:, :, None] * weight * block_step[None, :, :]
        local_part = jnp.einsum(
            "tsh,shp->thp", mixing, block_input, precision=lax.Precision.HIGHEST
        )
        carried = (
            jnp.einsum("tn,hpn->thp", block_out_map, ssm_state, precision=lax.Precision.HIGHEST)
            * jnp.exp(running)[:, :, None]
        )
        total_decay = running[-1]
        tail_weight = jnp.exp(total_decay[None, :] - running) * block_step
        new_state = ssm_state * jnp.exp(total_decay)[:, None, None] + jnp.einsum(
            "sh,shp,sn->hpn",
            tail_weight,
            block_input,
            block_in_map,
            precision=lax.Precision.HIGHEST,
        )
        return (new_state, local_part + carried)

    initial = jnp.zeros((HEADS, HDIM, STATE), jnp.float32)
    final_state, result = lax.scan(jax.checkpoint(ssd_one_block), initial, blocks)
    return result.reshape(length, HEADS, HDIM)


def mixer_core(
    projected,
    query_proj,
    key_proj,
    value_proj,
    conv_weight,
    conv_bias,
    decay_log,
    step_bias,
    skip_gain,
):
    length = projected.shape[0]
    inner_width = HEADS * HDIM
    channel_count = inner_width + 2 * STATE
    gate_z = projected[:, :inner_width]
    conv_in = projected[:, inner_width : inner_width + channel_count]
    step_raw = projected[:, inner_width + channel_count :]
    padded = jnp.pad(conv_in, ((CONV - 1, 0), (0, 0)))
    conv_out = conv_bias[None, :] + jnp.zeros_like(conv_in)
    for offset in range(CONV):
        conv_out = conv_out + conv_weight[offset][None, :] * padded[offset : offset + length]
    conv_act = jax.nn.silu(conv_out)
    ssm_input = conv_act[:, :inner_width].reshape(length, HEADS, HDIM)
    input_map = conv_act[:, inner_width : inner_width + STATE]
    output_map = conv_act[:, inner_width + STATE :]
    step_size = jax.nn.softplus(step_raw + step_bias[None, :])
    decay = -step_size * jnp.exp(decay_log)[None, :]
    ssm_out = (
        ssd_scan(ssm_input, step_size, decay, input_map, output_map)
        + skip_gain[None, :, None] * ssm_input
    )
    mamba_mixed = low(ssm_out.reshape(length, inner_width) * jax.nn.silu(gate_z))
    attended = low(low_back(attention_core(query_proj, key_proj, value_proj)))
    return (mamba_mixed, attended)


def on_device(
    tokens,
    lengths,
    mixer_gain,
    in_proj,
    conv_weight,
    conv_bias,
    decay_log,
    step_bias,
    skip_gain,
    query_weight,
    key_weight,
    value_weight,
    mamba_out,
    attn_out,
    mlp_gain,
    gate_weight,
    up_weight,
    down_weight,
    cotangent,
):
    row_count = tokens.shape[0]
    live_mask = (jnp.arange(row_count) < lengths[0]).astype(jnp.float32)[:, None]
    stream = tokens.astype(jnp.float32)
    mixer_full = (
        lax.all_gather(mixer_gain, "fsdp", axis=0, tiled=True),
        lax.all_gather(in_proj, "fsdp", axis=0, tiled=True),
        lax.all_gather(conv_weight, "fsdp", axis=1, tiled=True),
        lax.all_gather(conv_bias, "fsdp", axis=0, tiled=True),
        lax.all_gather(query_weight, "fsdp", axis=0, tiled=True),
        lax.all_gather(key_weight, "fsdp", axis=0, tiled=True),
        lax.all_gather(value_weight, "fsdp", axis=0, tiled=True),
        lax.all_gather(mamba_out, "fsdp", axis=0, tiled=True),
        lax.all_gather(attn_out, "fsdp", axis=0, tiled=True),
    )
    (
        gain_one,
        proj_full,
        conv_full,
        bias_full,
        query_full,
        key_full,
        value_full,
        mamba_full,
        attn_full,
    ) = mixer_full
    normed_float, norm_one_back = jax.vjp(norm_low, stream, gain_one.astype(jnp.float32))
    normed = normed_float.astype(jnp.bfloat16)
    projected = forward_product(normed, proj_full)
    query_proj = forward_product(normed, query_full)
    key_proj = forward_product(normed, key_full)
    value_proj = forward_product(normed, value_full)
    core_outputs, core_back = jax.vjp(
        mixer_core,
        projected,
        query_proj,
        key_proj,
        value_proj,
        conv_full.astype(jnp.float32),
        bias_full.astype(jnp.float32),
        decay_log,
        step_bias,
        skip_gain,
    )
    mamba_mixed = core_outputs[0].astype(jnp.bfloat16)
    attended = core_outputs[1].astype(jnp.bfloat16)
    mixed_stream = stream + live_mask * (
        forward_product(mamba_mixed, mamba_full) + forward_product(attended, attn_full)
    )
    mlp_full = (
        lax.all_gather(mlp_gain, "fsdp", axis=0, tiled=True),
        lax.all_gather(gate_weight, "fsdp", axis=0, tiled=True),
        lax.all_gather(up_weight, "fsdp", axis=0, tiled=True),
        lax.all_gather(down_weight, "fsdp", axis=0, tiled=True),
    )
    gain_two, gate_full, up_full, down_full = mlp_full
    normed_two_float, norm_two_back = jax.vjp(norm_low, mixed_stream, gain_two.astype(jnp.float32))
    normed_two = normed_two_float.astype(jnp.bfloat16)
    gate_value = forward_product(normed_two, gate_full)
    up_value = forward_product(normed_two, up_full)
    activated_float, unit_back = jax.vjp(gated_unit, gate_value, up_value)
    activated = activated_float.astype(jnp.bfloat16)
    output = (mixed_stream + live_mask * forward_product(activated, down_full)).astype(jnp.bfloat16)
    cot_stream = cotangent.astype(jnp.float32)
    gate_full, up_full, down_full = (
        lax.all_gather(gate_weight, "fsdp", axis=0, tiled=True),
        lax.all_gather(up_weight, "fsdp", axis=0, tiled=True),
        lax.all_gather(down_weight, "fsdp", axis=0, tiled=True),
    )
    branch_two = (live_mask * cot_stream).astype(jnp.bfloat16)
    grad_down = left_product(activated, branch_two)
    gate_float, up_float = unit_back(right_product(branch_two, down_full))
    gate_grad = gate_float.astype(jnp.bfloat16)
    up_grad = up_float.astype(jnp.bfloat16)
    grad_gate = left_product(normed_two, gate_grad)
    grad_up = left_product(normed_two, up_grad)
    normed_two_grad = right_product(gate_grad, gate_full) + right_product(up_grad, up_full)
    stream_two_grad, grad_gain_two = norm_two_back(normed_two_grad)
    mixed_grad = cot_stream + stream_two_grad
    mlp_shards = (
        lax.psum_scatter(
            grad_gain_two.astype(jnp.bfloat16), "fsdp", scatter_dimension=0, tiled=True
        ).astype(jnp.float32),
        lax.psum_scatter(
            grad_gate.astype(jnp.bfloat16), "fsdp", scatter_dimension=0, tiled=True
        ).astype(jnp.float32),
        lax.psum_scatter(
            grad_up.astype(jnp.bfloat16), "fsdp", scatter_dimension=0, tiled=True
        ).astype(jnp.float32),
        lax.psum_scatter(
            grad_down.astype(jnp.bfloat16), "fsdp", scatter_dimension=0, tiled=True
        ).astype(jnp.float32),
    )
    shard_gain_two, shard_gate, shard_up, shard_down = mlp_shards
    mlp_sums = (
        lax.psum(shard_gain_two.astype(jnp.bfloat16), "rep").astype(jnp.float32),
        lax.psum(shard_gate.astype(jnp.bfloat16), "rep").astype(jnp.float32),
        lax.psum(shard_up.astype(jnp.bfloat16), "rep").astype(jnp.float32),
        lax.psum(shard_down.astype(jnp.bfloat16), "rep").astype(jnp.float32),
    )
    out_gain_two, out_gate, out_up, out_down = mlp_sums
    proj_full, query_full, key_full, value_full, mamba_full, attn_full = (
        lax.all_gather(in_proj, "fsdp", axis=0, tiled=True),
        lax.all_gather(query_weight, "fsdp", axis=0, tiled=True),
        lax.all_gather(key_weight, "fsdp", axis=0, tiled=True),
        lax.all_gather(value_weight, "fsdp", axis=0, tiled=True),
        lax.all_gather(mamba_out, "fsdp", axis=0, tiled=True),
        lax.all_gather(attn_out, "fsdp", axis=0, tiled=True),
    )
    branch_one = (live_mask * mixed_grad).astype(jnp.bfloat16)
    grad_mamba = left_product(mamba_mixed, branch_one)
    grad_attn = left_product(attended, branch_one)
    core_grads = core_back(
        (right_product(branch_one, mamba_full), right_product(branch_one, attn_full))
    )
    (
        proj_float,
        query_float,
        key_float,
        value_float,
        conv_grad,
        bias_grad,
        decay_grad,
        step_grad,
        skip_grad,
    ) = core_grads
    proj_grad = proj_float.astype(jnp.bfloat16)
    query_grad = query_float.astype(jnp.bfloat16)
    key_grad = key_float.astype(jnp.bfloat16)
    value_grad = value_float.astype(jnp.bfloat16)
    grad_proj = left_product(normed, proj_grad)
    grad_query = left_product(normed, query_grad)
    grad_key = left_product(normed, key_grad)
    grad_value = left_product(normed, value_grad)
    normed_grad = (
        right_product(proj_grad, proj_full)
        + right_product(query_grad, query_full)
        + right_product(key_grad, key_full)
        + right_product(value_grad, value_full)
    )
    stream_one_grad, grad_gain_one = norm_one_back(normed_grad)
    grad_tokens = (mixed_grad + stream_one_grad).astype(jnp.bfloat16)
    mixer_shards = (
        lax.psum_scatter(grad_gain_one, "fsdp", scatter_dimension=0, tiled=True),
        lax.psum_scatter(grad_proj, "fsdp", scatter_dimension=0, tiled=True),
        lax.psum_scatter(conv_grad, "fsdp", scatter_dimension=1, tiled=True),
        lax.psum_scatter(bias_grad, "fsdp", scatter_dimension=0, tiled=True),
        lax.psum_scatter(grad_query, "fsdp", scatter_dimension=0, tiled=True),
        lax.psum_scatter(grad_key, "fsdp", scatter_dimension=0, tiled=True),
        lax.psum_scatter(grad_value, "fsdp", scatter_dimension=0, tiled=True),
        lax.psum_scatter(grad_mamba, "fsdp", scatter_dimension=0, tiled=True),
        lax.psum_scatter(grad_attn, "fsdp", scatter_dimension=0, tiled=True),
    )
    (
        shard_gain_one,
        shard_proj,
        shard_conv,
        shard_bias,
        shard_query,
        shard_key,
        shard_value,
        shard_mamba,
        shard_attn,
    ) = mixer_shards
    mixer_sums = lax.psum(
        (
            shard_gain_one,
            shard_proj,
            shard_conv,
            shard_bias,
            shard_query,
            shard_key,
            shard_value,
            shard_mamba,
            shard_attn,
        ),
        "rep",
    )
    (
        out_gain_one,
        out_proj,
        out_conv,
        out_bias,
        out_query,
        out_key,
        out_value,
        out_mamba,
        out_attn,
    ) = mixer_sums
    summed_per_head = lax.psum((decay_grad, step_grad, skip_grad), ("fsdp", "rep"))
    out_decay, out_step, out_skip = summed_per_head
    return (
        output,
        grad_tokens,
        out_gain_one,
        out_proj,
        out_conv,
        out_bias,
        out_decay,
        out_step,
        out_skip,
        out_query,
        out_key,
        out_value,
        out_mamba,
        out_attn,
        out_gain_two,
        out_gate,
        out_up,
        out_down,
    )


def solution(mesh):
    in_specs = (
        P(("fsdp", "rep"), None),
        P(("fsdp", "rep")),
        P("fsdp"),
        P("fsdp", None),
        P(None, "fsdp"),
        P("fsdp"),
        P(),
        P(),
        P(),
        P("fsdp", None),
        P("fsdp", None),
        P("fsdp", None),
        P("fsdp", None),
        P("fsdp", None),
        P("fsdp"),
        P("fsdp", None),
        P("fsdp", None),
        P("fsdp", None),
        P(("fsdp", "rep"), None),
    )
    out_specs = (
        P(("fsdp", "rep"), None),
        P(("fsdp", "rep"), None),
        P("fsdp"),
        P("fsdp", None),
        P(None, "fsdp"),
        P("fsdp"),
        P(),
        P(),
        P(),
        P("fsdp", None),
        P("fsdp", None),
        P("fsdp", None),
        P("fsdp", None),
        P("fsdp", None),
        P("fsdp"),
        P("fsdp", None),
        P("fsdp", None),
        P("fsdp", None),
    )
    return jax.shard_map(
        on_device, mesh=mesh, in_specs=in_specs, out_specs=out_specs, check_vma=False
    )
```

profile of v0, /device:TPU:11, one launch (start us, length us, event | category | flops | bytes accessed | tf_op | source)
XLA Modules:
  0.0 4650.6 jit_solution(17008871841799884703)
XLA Ops:
  13.6 14.6 all-gather
  34.1 23.8 all-gather.1
  60.1 14.5 all-reduce.20
  76.5 15.0 all-gather.2
  100.6 65.1 %all-gather.21.cloned.1.call-done = bf16[2048,1024]{1,0:T(8,128)(2,1)} async-done(((bf16[256,1024]{1,0:T(8,128)(2,1)}), bf16[2048,1024]{1,0:T(8,128)(2,1)}) %all-gather.21.cloned.1.call-update) | async-done | bytes 4194320 | tf_op jit(solution)/shard_map/all_gather | solution.py:244
  177.1 514.9 %all-gather.13.cloned.1.call-done = bf16[2048,6704]{0,1:T(8,128)(2,1)} async-done(((bf16[256,6704]{0,1:T(8,128)(2,1)}), bf16[2048,6704]{0,1:T(8,128)(2,1)}) %all-gather.13.cloned.1.call-update) | async-done | bytes 27459600 | tf_op jit(solution)/shard_map/all_gather | solution.py:241
  692.0 12.9 fusion.172
  710.6 12.6 fusion.95
  743.0 133.3 %while.54 = (s32[]{:T(128)}, f32[48,64,256]{2,1,0:T(8,128)S(1)}, f32[2,128,48,64]{1,0,3,2:T(2,128)}, f32[2,48,64,256]{3,2,1,0:T(8,128)}, f32[2,128,48]{2,1,0:T(8...) while((s32[]{:T(128)}, f32[48,64,256]{2,1,0:T(8,128)S(1)}, ...), condition=%wide.region_3.4_spmd.clone.clone, body=%wide.region_1.3_spmd.clone.clone.sunk | while | flops 3080067072 | bytes 27954988 | solution.py:175
  772.7 36.8 dynamic_update_slice.93
  839.1 36.8 dynamic_update_slice.93
  890.1 52.1 %all-gather.23.cloned.1.call-done = bf16[1024,2048]{1,0:T(8,128)(2,1)} async-done(((bf16[128,2048]{1,0:T(8,128)(2,1)}), bf16[1024,2048]{1,0:T(8,128)(2,1)}) %all-gather.23.cloned.1.call-update) | async-done | bytes 4194320 | tf_op jit(solution)/shard_map/all_gather | solution.py:248
  947.1 222.6 %all-gather.25.cloned.1.call-done = bf16[2048,4096]{1,0:T(8,128)(2,1)} async-done(((bf16[256,4096]{1,0:T(8,128)(2,1)}), bf16[2048,4096]{1,0:T(8,128)(2,1)}) %all-gather.25.cloned.1.call-update) | async-done | bytes 16777232 | tf_op jit(solution)/shard_map/all_gather | solution.py:286
  1169.7 10.1 fusion.175
  1179.8 217.8 %all-gather.27.cloned.1.call-done = bf16[2048,4096]{1,0:T(8,128)(2,1)} async-done(((bf16[256,4096]{1,0:T(8,128)(2,1)}), bf16[2048,4096]{1,0:T(8,128)(2,1)}) %all-gather.27.cloned.1.call-update) | async-done | bytes 16777232 | tf_op jit(solution)/shard_map/all_gather | solution.py:287
  1397.6 10.1 fusion.176
  1407.8 217.8 %all-gather.29.cloned.1.call-done = bf16[4096,2048]{1,0:T(8,128)(2,1)} async-done(((bf16[512,2048]{1,0:T(8,128)(2,1)}), bf16[4096,2048]{1,0:T(8,128)(2,1)}) %all-gather.29.cloned.1.call-update) | async-done | bytes 16777232 | tf_op jit(solution)/shard_map/all_gather | solution.py:288
  1625.6 13.5 multiply_convert_fusion
  1639.1 9.7 convolution_convert_fusion.2
  1648.9 10.0 convolution_convert_fusion.1
  1660.2 10.0 convolution_convert_fusion
  1675.9 12.4 fusion.177
  1688.3 14.3 multiply_reduce_fusion.9
  1742.8 10.2 fusion.180
  1753.7 13.2 multiply_reduce_fusion.8
  1776.4 254.6 %while.53 = (s32[]{:T(128)}, f32[48,64,256]{2,1,0:T(8,128)}, f32[2,128,48,64]{1,0,3,2:T(2,128)}, f32[2,128,48]{2,1,0:T(8,128)}, f32[2,128,48]{2,1,0:T(8,128)}, /...) while((s32[]{:T(128)}, f32[48,64,256]{2,1,0:T(8,128)}, ...), condition=%wide.region_18.19_spmd.clone, body=%wide.region_8.18_spmd.clone.sunk | while | flops 7423639552 | bytes 105451576 | solution.py:175
  1812.5 9.6 fusion.302
  1857.7 36.9 dynamic_update_slice.91
  1927.1 9.7 fusion.302
  1972.4 36.9 dynamic_update_slice.91
  2061.2 22.6 fusion.159
  2085.9 130.4 %reduce-scatter.27.cloned.1.call-done = bf16[256,4096]{1,0:T(8,128)(2,1)} async-done(((bf16[2048,4096]{1,0:T(8,128)(2,1)}), bf16[256,4096]{1,0:T(8,128)(2,1)}) %reduce-scatter.27.cloned.1.call-update) | async-done | bytes 2097168 | tf_op jit(solution)/shard_map/reduce_scatter | solution.py:321
  2216.4 285.4 %reduce-scatter.29.cloned.1.call-done = bf16[512,2048]{1,0:T(8,128)(2,1)} async-done(((bf16[4096,2048]{1,0:T(8,128)(2,1)}), bf16[512,2048]{1,0:T(8,128)(2,1)}) %reduce-scatter.29.cloned.1.call-update) | async-done | bytes 2097168 | tf_op jit(solution)/shard_map/reduce_scatter | solution.py:324
  2501.9 70.5 %reduce-scatter.17.cloned.1.call-done = f32[256,256]{1,0:T(8,128)} async-done(((f32[2048,256]{1,0:T(8,128)}), f32[256,256]{1,0:T(8,128)}) %reduce-scatter.17.cloned.1.call-update) | async-done | bytes 262160 | tf_op jit(solution)/shard_map/reduce_scatter | solution.py:383
  2572.3 70.6 %reduce-scatter.19.cloned.1.call-done = f32[256,256]{1,0:T(8,128)} async-done(((f32[2048,256]{1,0:T(8,128)}), f32[256,256]{1,0:T(8,128)}) %reduce-scatter.19.cloned.1.call-update) | async-done | bytes 262160 | tf_op jit(solution)/shard_map/reduce_scatter | solution.py:384
  2642.9 152.6 %reduce-scatter.15.cloned.1.call-done = f32[256,1024]{1,0:T(8,128)} async-done(((f32[2048,1024]{1,0:T(8,128)}), f32[256,1024]{1,0:T(8,128)}) %reduce-scatter.15.cloned.1.call-update) | async-done | bytes 1048592 | tf_op jit(solution)/shard_map/reduce_scatter | solution.py:382
  2795.5 151.5 %reduce-scatter.23.cloned.1.call-done = f32[128,2048]{1,0:T(8,128)} async-done(((f32[1024,2048]{1,0:T(8,128)}), f32[128,2048]{1,0:T(8,128)}) %reduce-scatter.23.cloned.1.call-update) | async-done | bytes 1048592 | tf_op jit(solution)/shard_map/reduce_scatter | solution.py:386
  2947.0 406.7 %reduce-scatter.21.cloned.1.call-done = f32[384,2048]{1,0:T(8,128)} async-done(((f32[3072,2048]{1,0:T(8,128)}), f32[384,2048]{1,0:T(8,128)}) %reduce-scatter.21.cloned.1.call-update) | async-done | bytes 3145744 | tf_op jit(solution)/shard_map/reduce_scatter | solution.py:385
  3353.8 856.7 %reduce-scatter.13.cloned.1.call-done = f32[256,6704]{0,1:T(8,128)} async-done(((f32[2048,6704]{0,1:T(8,128)}), f32[256,6704]{0,1:T(8,128)}) %reduce-scatter.13.cloned.1.call-update) | async-done | bytes 6864912 | tf_op jit(solution)/shard_map/reduce_scatter | solution.py:379
  4211.9 15.8 fusion.160
  4236.0 27.4 all-reduce.25
  4263.5 14.3 all-reduce.23
  4277.9 15.7 psum.124
  4294.4 43.0 all-reduce.24
  4342.3 9.5 fusion.101
  4352.8 11.4 all-reduce.26
  4364.3 40.6 all-reduce.34.cloned.1.call-done
  4414.1 217.6 %all-reduce.32.cloned.1.call-done = (f32[256,6704]{0,1:T(8,128)}, f32[256,1024]{1,0:T(8,128)}, f32[256,256]{1,0:T(8,128)}, f32[256,256]{1,0:T(8,128)}, f32[384,2048]{1,0:T(8,128)}, /*index=5*/f32[128,2048]{1,0:T(8,128)}) async-done(((f32[256,6704]{0,1:T(8,128)}, f32[256,1024]{1,0:T(8,128)}, f32[256,256]{1,0:T(8,128)}, f32[256,256]{1,0:T(8,128)}, f32[384,2048]{1,0:T(8,128)}, ...) | async-done | bytes 12632080 | tf_op jit(solution)/shard_map/psum | solution.py:399
  (520 shorter events, 397.8 us)
Async XLA Ops:
  7.2 88.5 %all-gather.19.cloned.1.call-start = ((), (), s32[]{:S(2)}) async-start(), calls=%async_computation.13 | async-start | bytes 1179648 | tf_op jit(solution)/shard_map/all_gather | solution.py:245
  7.9 90.6 %all-gather.17.cloned.1.call-start = ((), (), s32[]{:S(2)}) async-start(), calls=%async_computation.12 | async-start | bytes 1179648 | tf_op jit(solution)/shard_map/all_gather | solution.py:246
  8.7 157.0 %all-gather.21.cloned.1.call-start = ((), (), s32[]{:S(2)}) async-start(), calls=%async_computation.14 | async-start | bytes 4718592 | tf_op jit(solution)/shard_map/all_gather | solution.py:244
  9.4 682.6 %all-gather.13.cloned.1.call-start = ((), (), s32[]{:S(2)}) async-start(), calls=%async_computation.10 | async-start | bytes 30892032 | tf_op jit(solution)/shard_map/all_gather | solution.py:241
  10.0 871.7 %all-gather.15.cloned.1.call-start = ((), (), s32[]{:S(2)}) async-start(), calls=%async_computation.11 | async-start | bytes 14155776 | tf_op jit(solution)/shard_map/all_gather | solution.py:247
  10.6 931.6 %all-gather.23.cloned.1.call-start = ((), (), s32[]{:S(2)}) async-start(), calls=%async_computation.15 | async-start | bytes 4718592 | tf_op jit(solution)/shard_map/all_gather | solution.py:248
  11.2 1158.5 %all-gather.25.cloned.1.call-start = ((), (), s32[]{:S(2)}) async-start(), calls=%async_computation.16 | async-start | bytes 18874368 | tf_op jit(solution)/shard_map/all_gather | solution.py:286
  11.9 1385.7 %all-gather.27.cloned.1.call-start = ((), (), s32[]{:S(2)}) async-start(), calls=%async_computation.17 | async-start | bytes 18874368 | tf_op jit(solution)/shard_map/all_gather | solution.py:287
  12.7 45.9 copy-start.99
  12.7 47.2 %copy-start.100 = (bf16[448]{0:T(512)(128)(2,1)S(1)}, bf16[448]{0:T(512)(128)(2,1)}, u32[]{:S(2)}) copy-start(bf16[448]{0:T(512)(128)(2,1)} %param.28) | copy-start | bytes 2692
  12.7 63.8 %copy-start.103 = (bf16[256]{0:T(256)(128)(2,1)S(1)}, bf16[256]{0:T(256)(128)(2,1)}, u32[]{:S(2)}) copy-start(bf16[256]{0:T(256)(128)(2,1)} %param.37) | copy-start | bytes 1540
  12.7 1612.9 %all-gather.29.cloned.1.call-start = ((), (), s32[]{:S(2)}) async-start(), calls=%async_computation.18 | async-start | bytes 18874368 | tf_op jit(solution)/shard_map/all_gather | solution.py:288
  13.5 2072.5 %reduce-scatter.25.cloned.1.call-start = ((), (), s32[]{:S(2)}) async-start(), calls=%async_computation.25 | async-start | bytes 18874368 | tf_op jit(solution)/shard_map/reduce_scatter | solution.py:318
  75.6 22.9 copy-start.57
  75.6 22.9 copy-start.59
  75.7 94.0 %copy-start.45 = (f32[256,64]{1,0:T(8,128)}, f32[256,64]{1,0:T(8,128)S(1)}, u32[]{:S(2)}) copy-start(f32[256,64]{1,0:T(8,128)S(1)} %copy.238) | copy-start | bytes 196612
  75.8 93.9 %copy-start.47 = (f32[256,64]{1,0:T(8,128)}, f32[256,64]{1,0:T(8,128)S(1)}, u32[]{:S(2)}) copy-start(f32[256,64]{1,0:T(8,128)S(1)} %copy.237) | copy-start | bytes 196612
  95.7 614.9 %copy-start.66 = (f32[3584]{0:T(1024)}, f32[3584]{0:T(1024)S(1)}, u32[]{:S(2)}) copy-start(f32[3584]{0:T(1024)S(1)} %get-tuple-element.739) | copy-start | bytes 43012
  100.6 75.4 %copy-start.43 = (bf16[256,256]{0,1:T(8,128)(2,1)}, bf16[256,256]{0,1:T(8,128)(2,1)S(1)}, u32[]{:S(2)}) copy-start(bf16[256,256]{0,1:T(8,128)(2,1)S(1)} %convolution_convert_fusion.5) | copy-start | bytes 393220
  743.0 133.3 %copy-start.78 = (f32[3072]{0:T(1024)S(1)}, f32[3072]{0:T(1024)}, u32[]{:S(2)}) copy-start(f32[3072]{0:T(1024)} %mul.933) | copy-start | bytes 36868
  881.7 60.6 %copy-start.9 = (bf16[256,2048]{1,0:T(8,128)(2,1)S(1)}, bf16[256,2048]{1,0:T(8,128)(2,1)}, u32[]{:S(2)}) copy-start(bf16[256,2048]{1,0:T(8,128)(2,1)} %param.23) | copy-start | bytes 3145732
  881.7 60.5 %copy-start.87 = (f32[256]{0:T(256)S(1)}, f32[256]{0:T(256)}, u32[]{:S(2)}) copy-start(f32[256]{0:T(256)} %compare_convert_fusion) | copy-start | bytes 3076
  890.1 56.7 %copy-start.76 = (f32[8,1,256]{2,1,0:T(1,128)S(1)}, f32[8,1,256]{2,1,0:T(1,128)}, u32[]{:S(2)}) copy-start(f32[8,1,256]{2,1,0:T(1,128)} %convert_element_type.296) | copy-start | bytes 24580
  946.8 233.1 %copy-start.93 = (f32[256]{0:T(256)}, f32[256]{0:T(256)S(1)}, u32[]{:S(2)}) copy-start(f32[256]{0:T(256)S(1)} %get-tuple-element.860) | copy-start | bytes 3076
  946.8 755.9 %copy-start.5 = (f32[256,2048]{1,0:T(8,128)}, f32[256,2048]{1,0:T(8,128)S(1)}, u32[]{:S(2)}) copy-start(f32[256,2048]{1,0:T(8,128)S(1)} %get-tuple-element.861) | copy-start | bytes 6291460
  946.8 755.9 %copy-start.84 = (f32[256]{0:T(256)}, f32[256]{0:T(256)S(1)}, u32[]{:S(2)}) copy-start(f32[256]{0:T(256)S(1)} %fusion.152) | copy-start | bytes 3076
  1648.9 567.5 %reduce-scatter.27.cloned.1.call-start = ((), (), s32[]{:S(2)}) async-start(), calls=%async_computation.26 | async-start | bytes 18874368 | tf_op jit(solution)/shard_map/reduce_scatter | solution.py:321
  1659.0 842.8 %reduce-scatter.29.cloned.1.call-start = ((), (), s32[]{:S(2)}) async-start(), calls=%async_computation.27 | async-start | bytes 18874368 | tf_op jit(solution)/shard_map/reduce_scatter | solution.py:324
  1670.2 902.1 %reduce-scatter.17.cloned.1.call-start = ((), (), s32[]{:S(2)}) async-start(), calls=%async_computation.21 | async-start | bytes 2359296 | tf_op jit(solution)/shard_map/reduce_scatter | solution.py:383
  1719.9 923.0 %reduce-scatter.19.cloned.1.call-start = ((), (), s32[]{:S(2)}) async-start(), calls=%async_computation.22 | async-start | bytes 2359296 | tf_op jit(solution)/shard_map/reduce_scatter | solution.py:384
  1724.9 1070.7 %reduce-scatter.15.cloned.1.call-start = ((), (), s32[]{:S(2)}) async-start(), calls=%async_computation.20 | async-start | bytes 9437184 | tf_op jit(solution)/shard_map/reduce_scatter | solution.py:382
  1735.5 1211.5 %reduce-scatter.23.cloned.1.call-start = ((), (), s32[]{:S(2)}) async-start(), calls=%async_computation.24 | async-start | bytes 9437184 | tf_op jit(solution)/shard_map/reduce_scatter | solution.py:386
  1741.4 1612.4 %reduce-scatter.21.cloned.1.call-start = ((), (), s32[]{:S(2)}) async-start(), calls=%async_computation.23 | async-start | bytes 28311552 | tf_op jit(solution)/shard_map/reduce_scatter | solution.py:385
  1753.0 2457.5 %reduce-scatter.13.cloned.1.call-start = ((), (), s32[]{:S(2)}) async-start(), calls=%async_computation.19 | async-start | bytes 61784064 | tf_op jit(solution)/shard_map/reduce_scatter | solution.py:379
  1857.7 38.4 copy-start.15
  1857.7 38.4 copy-start.81
  1972.4 38.4 copy-start.15
  1972.4 38.4 copy-start.81
  2083.8 2267.9 %reduce-scatter.31.cloned.1.call-start = ((), (), s32[]{:S(2)}) async-start(), calls=%async_computation.28 | async-start | bytes 2064384
  2085.9 2319.0 %all-reduce.34.cloned.1.call-start = ((), (), s32[]{:S(2)}) async-start(), calls=%async_computation.30 | async-start | bytes 12582912 | tf_op jit(solution)/shard_map/psum | solution.py:331
  2501.8 2129.9 %all-reduce.32.cloned.1.call-start = ((), (), s32[]{:S(2)}) async-start(), calls=%async_computation.29 | async-start | bytes 25264128 | tf_op jit(solution)/shard_map/psum | solution.py:399
  4233.7 29.8 copy-start.96
  4233.7 60.7 %copy-start.105 = (f32[48]{0:T(128)S(1)}, f32[48]{0:T(128)}, u32[]{:S(2)}) copy-start(f32[48]{0:T(128)} %param.29) | copy-start | bytes 580
  4233.7 103.6 %copy-start.92 = (f32[256]{0:T(256)S(1)}, f32[256]{0:T(256)}, u32[]{:S(2)}) copy-start(f32[256]{0:T(256)} %copy-done.91) | copy-start | bytes 3076
  4233.7 103.6 %copy-start.6 = (f32[256,2048]{1,0:T(8,128)S(1)}, f32[256,2048]{1,0:T(8,128)}, u32[]{:S(2)}) copy-start(f32[256,2048]{1,0:T(8,128)} %copy-done.5) | copy-start | bytes 6291460
  4233.7 103.6 %copy-start.77 = (f32[8,1,256]{2,1,0:T(1,128)S(1)}, f32[8,1,256]{2,1,0:T(1,128)}, u32[]{:S(2)}) copy-start(f32[8,1,256]{2,1,0:T(1,128)} %convert_element_type.296) | copy-start | bytes 24580
  4233.7 103.6 %copy-start.85 = (f32[256]{0:T(256)S(1)}, f32[256]{0:T(256)}, u32[]{:S(2)}) copy-start(f32[256]{0:T(256)} %copy-done.84) | copy-start | bytes 3076
  4233.7 103.6 %copy-start.90 = (f32[256]{0:T(256)S(1)}, f32[256]{0:T(256)}, u32[]{:S(2)}) copy-start(f32[256]{0:T(256)} %copy-done.89) | copy-start | bytes 3076
  (95 other events, 451.7 us)
Sparse Core Ops, SparseCore 0:
  10.2 39.8 all-gather.18
  52.2 39.0 all-gather.16
  93.4 72.2 all-gather.20
  167.0 524.9 all-gather.12
  694.0 173.9 all-gather.14
  870.0 72.1 all-gather.22
  944.3 225.2 all-gather.24
  1171.8 225.7 all-gather.26
  1399.7 225.7 all-gather.28
  1649.0 281.2 reduce-scatter.24
  1934.6 281.7 reduce-scatter.26
  2220.0 281.7 reduce-scatter.28
  2505.7 66.5 reduce-scatter.16
  2576.1 66.7 reduce-scatter.18
  2646.8 148.6 reduce-scatter.14
  2799.0 147.9 reduce-scatter.22
  2951.3 402.4 reduce-scatter.20
  3357.7 852.7 reduce-scatter.12
  4214.6 65.6 reduce-scatter.30
  4282.9 121.9 all-reduce.33
  4408.2 223.4 all-reduce.31
where the time goes:
time: 4670 us; the launch traced here: 4650 us
  waiting for transfers between devices  3680 us (79%)
  matrix products  354 us (8%)
  local copies, waits for them, and re-layouts  285 us (6%)
  blocking collectives  180 us (4%)
  other arithmetic  105 us (2%)
    reduce_scatter x1, waiting for transfers between devices, on_device(): lax.psum_scatter(grad_proj, 'fsdp', scatter_dimension=0, tiled=True)  857 us
    all_gather x1, waiting for transfers between devices, on_device(): lax.all_gather(in_proj, 'fsdp', axis=0, tiled=True)  515 us
    reduce_scatter x1, waiting for transfers between devices, on_device(): lax.psum_scatter(grad_mamba, 'fsdp', scatter_dimension=0, tiled=True)  407 us
    reduce_scatter x1, waiting for transfers between devices, on_device(): lax.psum_scatter(grad_down.astype(jnp.bfloat16), 'fsdp', scatter_dimensio...  285 us
    all_gather x1, waiting for transfers between devices, on_device(): lax.all_gather(gate_weight, 'fsdp', axis=0, tiled=True)  223 us
    all_gather x1, waiting for transfers between devices, on_device(): lax.all_gather(down_weight, 'fsdp', axis=0, tiled=True)  218 us
    all_gather x1, waiting for transfers between devices, on_device(): lax.all_gather(up_weight, 'fsdp', axis=0, tiled=True)  218 us
    psum x1, waiting for transfers between devices, on_device(): lax.psum((shard_gain_one, shard_proj, shard_conv, shard_bias, shard_query...  218 us
  transfers between devices with their start and end apart: 21, of which 16 were waited for; matrix products, arithmetic and copies ran while one was open for 15% of the time, Pallas kernels for 0%

commit v1 on v0

v1 whole, which is shorter than its diff:
```python
import functools

import jax
import jax.numpy as jnp
from jax import lax
from jax.experimental import pallas as pl
from jax.experimental.pallas import tpu as pltpu
from jax.sharding import PartitionSpec as P

HEADS = 48
HDIM = 64
STATE = 256
CONV = 4
QH = 8
KVH = 2
HEAD_WIDTH = 128
INNER = HEADS * HDIM
LANES = 128
ROWS = 128
MIB = 1 << 20
MESH = pl.DeviceIdType.MESH

epsilon = 1e-05
BF16 = jnp.bfloat16
F32 = jnp.float32
HIGHEST = lax.Precision.HIGHEST


def dot(left, right, contract=((1,), (0,)), precision=None):
    return lax.dot_general(
        left, right, (contract, ((), ())), preferred_element_type=F32, precision=precision
    )


def dot_tn(left, right, precision=None):
    return dot(left, right, ((0,), (0,)), precision)


def dot_nt(left, right, precision=None):
    return dot(left, right, ((1,), (1,)), precision)


def sigmoid(v):
    return 1.0 / (1.0 + jnp.exp(-v))


def silu_slope(v, sig):
    return sig * (1.0 + v * (1.0 - sig))


def softplus(v):
    return jnp.maximum(v, 0.0) + jnp.log1p(jnp.exp(-jnp.abs(v)))


def shift_down(v, by):
    if by == 0:
        return v
    return jnp.concatenate([jnp.zeros((by, v.shape[1]), v.dtype), v[:-by]], axis=0)


def shift_up(v, by):
    if by == 0:
        return v
    return jnp.concatenate([v[by:], jnp.zeros((by, v.shape[1]), v.dtype)], axis=0)


class Cut:
    def __init__(self, reps):
        self.heads = HEADS // reps
        self.inner = INNER // reps
        self.qheads = QH // reps
        self.qwidth = self.qheads * HEAD_WIDTH
        self.q = 0
        self.step = self.qwidth
        self.z = self.step + LANES
        self.x = self.z + self.inner
        self.maps = self.x + self.inner
        self.k = self.maps + 2 * STATE
        self.v = self.k + HEAD_WIDTH
        self.width = self.v + HEAD_WIDTH
        self.conv = self.inner + 2 * STATE
        self.shared = (self.width - self.maps) // 2
        self.way = (self.maps + self.shared) // 2

    def ring_row(self, column):
        half = self.maps // 2
        return column if column < half else column - half + self.way


def conv_out_of(ref, lanes, start, conv_ref):
    width = lanes.stop - lanes.start
    given = ref[:, start : start + width].astype(F32)
    total = conv_ref[CONV : CONV + 1, lanes]
    for tap in range(CONV):
        total = total + conv_ref[tap : tap + 1, lanes] * shift_down(given, CONV - 1 - tap)
    return total, given


def conv_back(d_out, given, conv_ref, lanes, sums_ref):
    d_given = jnp.zeros_like(d_out)
    for tap in range(CONV):
        back = CONV - 1 - tap
        d_given = d_given + conv_ref[tap : tap + 1, lanes] * shift_up(d_out, back)
        sums_ref[tap : tap + 1, lanes] += jnp.sum(
            d_out * shift_down(given, back), axis=0, keepdims=True
        )
    sums_ref[CONV : CONV + 1, lanes] += jnp.sum(d_out, axis=0, keepdims=True)
    return d_given


def ones_triangle(length, upper):
    row = lax.broadcasted_iota(jnp.int32, (length, length), 0)
    col = lax.broadcasted_iota(jnp.int32, (length, length), 1)
    return jnp.where(col >= row if upper else col <= row, 1.0, 0.0).astype(F32)


def steps_of(step_ref, head_ref):
    raw = step_ref[...] + head_ref[1:2, :]
    step = softplus(raw)
    decay = -step * jnp.exp(head_ref[0:1, :])
    running = dot(ones_triangle(raw.shape[0], False), decay, precision=HIGHEST)
    return raw, step, decay, running


def decay_block(running, running_t, head, block):
    top, width = block * ROWS, (block + 1) * ROWS
    gap = running[top:width, head : head + 1] - running_t[head : head + 1, :width]
    row = lax.broadcasted_iota(jnp.int32, (ROWS, width), 0) + top
    col = lax.broadcasted_iota(jnp.int32, (ROWS, width), 1)
    return jnp.where(row >= col, jnp.exp(gap), 0.0)


def turn(v, cos_ref, sin_ref):
    half = HEAD_WIDTH // 2
    return v * cos_ref[...] + pltpu.roll(v, half, 1) * sin_ref[...]


def turn_back(v, cos_ref, sin_ref):
    half = HEAD_WIDTH // 2
    return v * cos_ref[...] - pltpu.roll(v, half, 1) * sin_ref[...]


def softmax_rows(q, k):
    scores = dot_nt(q, k) * HEAD_WIDTH ** (-0.5)
    row = lax.broadcasted_iota(jnp.int32, scores.shape, 0)
    col = lax.broadcasted_iota(jnp.int32, scores.shape, 1)
    scores = jnp.where(row >= col, scores, -1e30)
    top = jnp.max(scores, axis=1, keepdims=True)
    weight = jnp.exp(scores - top)
    return weight / jnp.sum(weight, axis=1, keepdims=True)


def mixer_forward(
    cut, proj_ref, step_ref, conv_ref, head_ref, chan_ref, cos_ref, sin_ref, out_ref, act_ref
):
    length = proj_ref.shape[0]
    for lane in range(0, cut.conv, 2 * LANES):
        lanes = slice(lane, min(lane + 2 * LANES, cut.conv))
        total, _ = conv_out_of(proj_ref, lanes, cut.x + lane, conv_ref)
        act_ref[:, lanes] = total * sigmoid(total)
    _, step, _, running = steps_of(step_ref, head_ref)
    step_t, running_t = step.T, running.T
    in_map = act_ref[:, cut.inner : cut.inner + STATE].astype(BF16)
    out_map = act_ref[:, cut.inner + STATE : cut.inner + 2 * STATE].astype(BF16)
    pairing = dot_nt(out_map, in_map)
    first = lax.broadcasted_iota(jnp.int32, (ROWS, LANES), 1) < HDIM
    for pair in range(cut.heads // 2):
        lanes = slice(pair * LANES, (pair + 1) * LANES)
        given = act_ref[:, lanes].astype(BF16)
        for block in range(length // ROWS):
            rows = slice(block * ROWS, (block + 1) * ROWS)
            parts = []
            for head in (2 * pair, 2 * pair + 1):
                mixing = (
                    pairing[rows, : rows.stop]
                    * decay_block(running, running_t, head, block)
                    * step_t[head : head + 1, : rows.stop]
                )
                parts.append(dot(mixing.astype(BF16), given[: rows.stop]))
            ssm = jnp.where(first, parts[0], parts[1])
            ssm = ssm + chan_ref[0:1, lanes] * act_ref[rows, lanes]
            gate = proj_ref[rows, cut.z + lanes.start : cut.z + lanes.stop].astype(F32)
            out_ref[rows, lanes] = (ssm * gate * sigmoid(gate)).astype(BF16)
    key = turn(proj_ref[:, cut.k : cut.k + HEAD_WIDTH].astype(F32), cos_ref, sin_ref).astype(BF16)
    value = proj_ref[:, cut.v : cut.v + HEAD_WIDTH].astype(BF16)
    for head in range(cut.qheads):
        at = cut.q + head * HEAD_WIDTH
        query = turn(proj_ref[:, at : at + HEAD_WIDTH].astype(F32), cos_ref, sin_ref).astype(BF16)
        probs = softmax_rows(query, key).astype(BF16)
        to = cut.inner + head * HEAD_WIDTH
        out_ref[:, to : to + HEAD_WIDTH] = dot(probs, value).astype(BF16)


def mixer_backward(
    cut,
    proj_ref,
    step_ref,
    grad_ref,
    conv_ref,
    head_ref,
    chan_ref,
    cos_ref,
    sin_ref,
    d_ref,
    conv_sum_ref,
    head_sum_ref,
    chan_sum_ref,
    act_ref,
    d_act_ref,
    d_pair_ref,
    col_ref,
):
    length = proj_ref.shape[0]

    for lane in range(0, cut.conv, 2 * LANES):
        lanes = slice(lane, min(lane + 2 * LANES, cut.conv))
        total, _ = conv_out_of(proj_ref, lanes, cut.x + lane, conv_ref)
        act_ref[:, lanes] = total * sigmoid(total)
    raw, step, decay, running = steps_of(step_ref, head_ref)
    step_t, running_t = step.T, running.T
    in_map = act_ref[:, cut.inner : cut.inner + STATE].astype(BF16)
    out_map = act_ref[:, cut.inner + STATE : cut.inner + 2 * STATE].astype(BF16)
    pairing = dot_nt(out_map, in_map)
    d_pair_ref[...] = jnp.zeros_like(d_pair_ref)
    col_ref[...] = jnp.zeros_like(col_ref)
    first = lax.broadcasted_iota(jnp.int32, (ROWS, LANES), 1) < HDIM
    lane_of = lax.broadcasted_iota(jnp.int32, (ROWS, LANES), 1)
    row_sums = [jnp.zeros((ROWS, LANES), F32) for _ in range(length // ROWS)]
    for pair in range(cut.heads // 2):
        lanes = slice(pair * LANES, (pair + 1) * LANES)
        given_f = act_ref[:, lanes]
        given = given_f.astype(BF16)
        skip = chan_ref[0:1, lanes]
        skip_sum = jnp.zeros((1, LANES), F32)
        for block in range(length // ROWS):
            rows = slice(block * ROWS, (block + 1) * ROWS)
            width = rows.stop
            z_lanes = slice(cut.z + lanes.start, cut.z + lanes.stop)
            gate = proj_ref[rows, z_lanes].astype(F32)
            sig = sigmoid(gate)
            d_mixed = grad_ref[rows, lanes].astype(F32)
            d_ssm = d_mixed * gate * sig
            skip_sum = skip_sum + jnp.sum(d_ssm * given_f[rows], axis=0, keepdims=True)
            parts = []
            d_given = jnp.zeros((width, LANES), F32)
            for which in range(2):
                head = 2 * pair + which
                d_head = jnp.where(first if which == 0 else ~first, d_ssm, 0.0).astype(BF16)
                fall = decay_block(running, running_t, head, block)
                step_row = step_t[head : head + 1, :width]
                d_mixing = dot_nt(d_head, given[:width])
                stepped = fall * step_row
                mixing = pairing[rows, :width] * stepped
                mixing_low = mixing.astype(BF16)
                parts.append(dot(mixing_low, given[:width]))
                d_given = d_given + dot_tn(mixing_low, d_head)
                d_pair_ref[rows, :width] += d_mixing * stepped
                flow = d_mixing * mixing
                row_sums[block] = jnp.where(
                    lane_of == head,
                    jnp.sum(flow, axis=1, keepdims=True),
                    row_sums[block],
                )
                col_ref[head : head + 1, :width] += jnp.sum(
                    d_mixing * pairing[rows, :width] * fall, axis=0, keepdims=True
                )
            if block == 0:
                d_act_ref[:, lanes] = jnp.zeros((length, LANES), F32)
            d_act_ref[:width, lanes] += d_given
            d_act_ref[rows, lanes] += d_ssm * skip
            ssm = jnp.where(first, parts[0], parts[1]) + skip * given_f[rows]
            d_ref[rows, z_lanes] = (d_mixed * ssm * silu_slope(gate, sig)).astype(BF16)
        chan_sum_ref[0:1, lanes] += skip_sum
    d_pair = d_pair_ref[...].astype(BF16)
    d_act_ref[:, cut.inner : cut.inner + STATE] = dot_tn(d_pair, out_map)
    d_act_ref[:, cut.inner + STATE : cut.inner + 2 * STATE] = dot(d_pair, in_map)
    col_sum = col_ref[...].T
    d_running = jnp.concatenate(row_sums, axis=0) - step * col_sum
    d_decay = dot(ones_triangle(length, True), d_running, precision=HIGHEST)
    d_step = col_sum - d_decay * jnp.exp(head_ref[0:1, :])
    d_raw = d_step * sigmoid(raw)
    valid = lax.broadcasted_iota(jnp.int32, d_raw.shape, 1) < cut.heads
    d_raw = jnp.where(valid, d_raw, 0.0)
    d_ref[:, cut.step : cut.step + LANES] = d_raw.astype(BF16)
    head_sum_ref[0:1, :] += jnp.sum(d_decay * decay, axis=0, keepdims=True)
    head_sum_ref[1:2, :] += jnp.sum(d_raw, axis=0, keepdims=True)
    for lane in range(0, cut.conv, 2 * LANES):
        lanes = slice(lane, min(lane + 2 * LANES, cut.conv))
        total, given = conv_out_of(proj_ref, lanes, cut.x + lane, conv_ref)
        d_out = d_act_ref[:, lanes] * silu_slope(total, sigmoid(total))
        d_given = conv_back(d_out, given, conv_ref, lanes, conv_sum_ref)
        d_ref[:, cut.x + lane : cut.x + lanes.stop] = d_given.astype(BF16)
    key = turn(proj_ref[:, cut.k : cut.k + HEAD_WIDTH].astype(F32), cos_ref, sin_ref).astype(BF16)
    value = proj_ref[:, cut.v : cut.v + HEAD_WIDTH].astype(BF16)
    d_key = jnp.zeros((length, HEAD_WIDTH), F32)
    d_value = jnp.zeros((length, HEAD_WIDTH), F32)
    for head in range(cut.qheads):
        at = cut.q + head * HEAD_WIDTH
        query = turn(proj_ref[:, at : at + HEAD_WIDTH].astype(F32), cos_ref, sin_ref).astype(BF16)
        probs = softmax_rows(query, key)
        to = cut.inner + head * HEAD_WIDTH
        d_attended = grad_ref[:, to : to + HEAD_WIDTH].astype(BF16)
        d_probs = dot_nt(d_attended, value)
        inner = jnp.sum(probs * d_probs, axis=1, keepdims=True)
        d_scores = (probs * (d_probs - inner)).astype(BF16)
        d_query = dot(d_scores, key) * HEAD_WIDTH ** (-0.5)
        d_key = d_key + dot_tn(d_scores, query) * HEAD_WIDTH ** (-0.5)
        d_value = d_value + dot_tn(probs.astype(BF16), d_attended)
        d_ref[:, at : at + HEAD_WIDTH] = turn_back(d_query, cos_ref, sin_ref).astype(BF16)
    d_ref[:, cut.k : cut.k + HEAD_WIDTH] = turn_back(d_key, cos_ref, sin_ref).astype(BF16)
    d_ref[:, cut.v : cut.v + HEAD_WIDTH] = d_value.astype(BF16)


def spread(moves, places_ref, blocks_ref, *refs):
    for which in range(4):
        at = places_ref[which]
        for out, rows, lanes, row_by, lane_by, lane_from in moves:
            height, width = rows.stop - rows.start, lanes.stop - lanes.start
            row, lane = at * row_by, lane_from + at * lane_by
            if row_by:
                row = pl.multiple_of(row, row_by)
            if lane_by and lane_by % LANES == 0:
                lane = pl.multiple_of(lane, LANES)
            refs[out][pl.ds(row, height), pl.ds(lane, width)] = blocks_ref[
                which, rows, lanes
            ].astype(F32)


def spread_call(places, blocks, outs, moves):
    if any(move[4] % LANES for move in moves):
        return spread_plain(places, blocks, outs, moves)
    return pl.pallas_call(
        functools.partial(spread, moves),
        out_shape=[jax.ShapeDtypeStruct(shape, F32) for shape in outs],
        in_specs=[pl.BlockSpec(memory_space=pltpu.SMEM)]
        + [pl.BlockSpec(memory_space=pltpu.VMEM)],
        out_specs=[pl.BlockSpec(memory_space=pltpu.VMEM)] * len(outs),
        compiler_params=pltpu.CompilerParams(vmem_limit_bytes=40 * MIB),
        name="spread",
    )(places, blocks)


def spread_plain(places, blocks, outs, moves):
    result = [jnp.zeros(shape, F32) for shape in outs]
    for which in range(4):
        block, at = blocks[which], places[which]
        for out, rows, lanes, row_by, lane_by, lane_from in moves:
            result[out] = lax.dynamic_update_slice(
                result[out],
                block[rows, lanes].astype(F32),
                (at * row_by, lane_from + at * lane_by),
            )
    return result


def spread_in(cut, places_ref, *refs):
    blocks_ref, wide_ref, query_ref, key_ref, value_ref = refs
    key_ref[...] = jnp.zeros_like(key_ref)
    value_ref[...] = jnp.zeros_like(value_ref)
    split = cut.maps // 2
    first = split - cut.z
    maps = 2 * INNER
    for which in range(4):
        block = blocks_ref.at[which]
        at = places_ref[which]
        lanes = pl.ds(pl.multiple_of(at * cut.qwidth, LANES), cut.qwidth)
        query_ref[:, lanes] = block[: cut.qwidth].astype(F32).T
        to = pl.multiple_of(at * cut.inner, ROWS)
        wide_ref[pl.ds(to, first)] = block[cut.z : split].astype(F32)
        wide_ref[pl.ds(pl.multiple_of(to + first, 64), cut.inner - first)] = block[
            cut.way : cut.way + cut.inner - first
        ].astype(F32)
        wide_ref[pl.ds(INNER + to, cut.inner)] = block[
            cut.way + cut.inner - first : cut.way + split
        ].astype(F32)
    halves = [
        jnp.concatenate(
            [
                blocks_ref[which, split : cut.way].astype(F32),
                blocks_ref[which, cut.way + split :].astype(F32),
            ],
            axis=0,
        )
        for which in range(4)
    ]
    ones = [places_ref[which] % 2 for which in range(4)]
    low_half = sum(jnp.where(one == 0, half, 0.0) for one, half in zip(ones, halves))
    wide_ref[maps : maps + cut.shared] = low_half
    rest = 2 * STATE - cut.shared
    high = [jnp.where(one == 1, half, 0.0) for one, half in zip(ones, halves)]
    wide_ref[maps + cut.shared : maps + 2 * STATE] = sum(half[:rest] for half in high)
    for which, half in enumerate(high):
        lanes = pl.ds(
            pl.multiple_of(places_ref[which] * KVH // 4 * HEAD_WIDTH, LANES), HEAD_WIDTH
        )
        key_ref[:, lanes] += half[rest : rest + HEAD_WIDTH].T
        value_ref[:, lanes] += half[rest + HEAD_WIDTH :].T
    for rep in range(4):
        steps = sum(
            jnp.where(places_ref[which] == rep, 1.0, 0.0)
            * blocks_ref[which, cut.step : cut.step + LANES].astype(F32)
            for which in range(4)
        )
        to = maps + 2 * STATE + rep * cut.heads
        wide_ref[to : to + cut.heads] = steps[: cut.heads]


def spread_in_call(cut, places, blocks):
    depth = blocks.shape[2]
    vmem = pl.BlockSpec(memory_space=pltpu.VMEM)
    columns_in = 2 * INNER + 2 * STATE + HEADS
    return pl.pallas_call(
        functools.partial(spread_in, cut),
        out_shape=[
            jax.ShapeDtypeStruct((columns_in, depth), F32),
            jax.ShapeDtypeStruct((depth, QH * HEAD_WIDTH), F32),
            jax.ShapeDtypeStruct((depth, KVH * HEAD_WIDTH), F32),
            jax.ShapeDtypeStruct((depth, KVH * HEAD_WIDTH), F32),
        ],
        in_specs=[pl.BlockSpec(memory_space=pltpu.SMEM), vmem],
        out_specs=[vmem] * 4,
        compiler_params=pltpu.CompilerParams(vmem_limit_bytes=40 * MIB),
        name="spread_in",
    )(places, blocks)


def turn_tables(length):
    half = HEAD_WIDTH // 2
    position = jnp.arange(length).astype(F32)
    freqs = 10000.0 ** (-jnp.arange(half).astype(F32) * 2.0 / HEAD_WIDTH)
    angles = position[:, None] * freqs[None, :]
    cosine, sine = jnp.cos(angles), jnp.sin(angles)
    return (
        jnp.concatenate([cosine, cosine], axis=1),
        jnp.concatenate([-sine, sine], axis=1),
    )


class Ring:
    def __init__(self, shards):
        self.shards = shards
        self.index = lax.axis_index("fsdp")
        self.place = ring_place(self.index, shards)

    def at(self, offset):
        return ring_at(self.place + offset, self.shards)

    def peer(self, way):
        return {"fsdp": self.at(1 - 2 * way)}


class Pair:
    def __init__(self):
        self.rep = lax.axis_index("rep")
        across, core = self.rep // 2, self.rep % 2
        self.peers = ({"rep": (1 - across) * 2 + core}, {"rep": across * 2 + 1 - core})
        self.corner = {"rep": (1 - across) * 2 + 1 - core}


def greet(ring, pair, *more, maybe=(), are=None):
    barrier = pltpu.get_barrier_semaphore()

    def signal(peers):
        for peer in peers:
            pl.semaphore_signal(barrier, inc=1, device_id=peer, device_id_type=MESH)

    peers = (ring.peer(0), ring.peer(1)) + pair.peers + more
    signal(peers)
    if not maybe:
        pl.semaphore_wait(barrier, len(peers))
        return
    pl.when(are == 1)(lambda: signal(maybe))
    pl.semaphore_wait(barrier, len(peers) + len(maybe) * are)


class Gather:
    def __init__(self, ring, ways, send, recv, hook=None):
        self.ring, self.ways, self.send, self.recv = ring, ways, send, recv
        self.hook = hook or (lambda step, way, piece: None)

    def pieces(self):
        for piece in range(max(len(way) for way in self.ways)):
            for way in range(2):
                if piece < len(self.ways[way]):
                    yield way, piece

    def copy(self, step, way, piece, first=False):
        own, place = self.ways[way][piece]
        there = place(self.ring.at((2 * way - 1) * (step - 1)))
        return pltpu.make_async_remote_copy(
            src_ref=own if first else there,
            dst_ref=there,
            send_sem=self.send.at[step - 1, way, piece],
            recv_sem=self.recv.at[step - 1, way, piece],
            device_id=self.ring.peer(way),
            device_id_type=MESH,
        )

    def landed(self, step, way, piece):
        here = self.ways[way][piece][1](self.ring.at((2 * way - 1) * step))
        return pltpu.make_async_remote_copy(
            src_ref=here,
            dst_ref=here,
            send_sem=self.send.at[step - 1, way, piece],
            recv_sem=self.recv.at[step - 1, way, piece],
            device_id=self.ring.peer(way),
            device_id_type=MESH,
        )

    def start(self):
        for way, piece in self.pieces():
            self.copy(1, way, piece, True).start()

    def advance(self, step):
        for way, piece in self.pieces():
            self.landed(step - 1, way, piece).wait_recv()
            self.copy(step, way, piece).start()
            self.hook(step - 1, way, piece)

    def run(self, first, stop):
        def body(step, carry):
            self.advance(step)
            return carry

        lax.fori_loop(first, stop, body, 0)

    def finish(self):
        for way, piece in self.pieces():
            self.landed(self.ring.shards - 1, way, piece).wait_recv()
            self.hook(self.ring.shards - 1, way, piece)
            self.copy(1, way, piece, True).wait_send()

        def body(step, carry):
            for way, piece in self.pieces():
                self.copy(step, way, piece).wait_send()
            return carry

        lax.fori_loop(2, self.ring.shards, body, 0)


def ring_sems(shards, pieces):
    return [pltpu.SemaphoreType.DMA((shards - 1, 2, pieces))] * 2


def remote(src, dst, send, recv, peer):
    return pltpu.make_async_remote_copy(
        src_ref=src, dst_ref=dst, send_sem=send, recv_sem=recv, device_id=peer, device_id_type=MESH
    )


def block_at(ref, index, rows, lanes):
    if len(ref.shape) == 2:
        return ref.at[rows, pl.ds(pl.multiple_of(index * lanes, LANES), lanes)]
    return ref.at[index, rows]


def gather_in(shards, cut, inside, *refs):
    refs = list(refs)
    take = lambda number: [refs.pop(0) for _ in range(number)]
    in_ref, query_ref, key_ref, value_ref, aux_ref, tokens_ref, cot_ref, live_ref = take(8)
    w_ref, aux_all_ref, branch_all_ref = take(3)
    if inside:
        normed_ref, proj_ref, steps_ref = take(3)
    else:
        (tokens_all_ref,) = take(1)
    share_ref, turn_ref, rows_ref, branch_ref = take(4)
    pack_sem, send, recv, core_send, core_recv = take(5)
    token_sems, branch_sems = take(3), take(3)
    if inside:
        sum_ref, scale_ref, w_sem, w_out_ref = take(4)
        w_ref, w_out_ref = w_out_ref, w_ref
        tokens_all_ref = take(1)[0]

    ring, pair = Ring(shards), Pair()
    rep, core = pair.rep, pair.rep % 2
    depth = in_ref.shape[1]
    copies = (
        (
            in_ref.at[pl.ds(pl.multiple_of(cut.inner * rep, ROWS), cut.inner)],
            share_ref.at[pl.ds(cut.z, cut.inner)],
        ),
        (
            in_ref.at[pl.ds(pl.multiple_of(INNER + cut.inner * rep, ROWS), cut.inner)],
            share_ref.at[pl.ds(cut.x, cut.inner)],
        ),
        (
            in_ref.at[pl.ds(2 * INNER, 2 * STATE)],
            share_ref.at[pl.ds(cut.maps, 2 * STATE)],
        ),
        (in_ref.at[pl.ds(2 * INNER + 2 * STATE, HEADS)], rows_ref),
        (
            query_ref.at[:, pl.ds(pl.multiple_of(cut.qwidth * rep, LANES), cut.qwidth)],
            turn_ref.at[:, pl.ds(0, cut.qwidth)],
        ),
    ) + tuple(
        (
            ref.at[:, pl.ds(pl.multiple_of(rep * KVH // 4 * HEAD_WIDTH, LANES), HEAD_WIDTH)],
            turn_ref.at[:, pl.ds(cut.qwidth + number * HEAD_WIDTH, HEAD_WIDTH)],
        )
        for number, ref in enumerate((key_ref, value_ref))
    )
    packs = [
        pltpu.make_async_copy(src, dst, pack_sem.at[number])
        for number, (src, dst) in enumerate(copies)
    ]
    for pack in packs:
        pack.start()
    greet(ring, pair)
    branch_ref[...] = (cot_ref[...].astype(F32) * live_ref[:, 0:1]).astype(BF16)
    for pack in packs:
        pack.wait()
    share_ref[: cut.qwidth] = turn_ref[:, : cut.qwidth].T
    share_ref[cut.k :] = turn_ref[:, cut.qwidth :].T
    row = lax.broadcasted_iota(jnp.int32, (LANES, HEADS), 0)
    column = lax.broadcasted_iota(jnp.int32, (LANES, HEADS), 1)
    chosen = jnp.logical_and(column == row + cut.heads * rep, row < cut.heads)
    chosen = jnp.where(chosen, 1.0, 0.0).astype(BF16)
    share_ref[cut.step : cut.z] = dot(chosen, rows_ref[...]).astype(BF16)
    every = pl.ds(0, cut.width)
    keeps = [
        pltpu.make_async_copy(src, dst, pack_sem.at[len(packs) + number])
        for number, (src, dst) in enumerate(
            (
                (share_ref, block_at(w_ref, ring.index, every, depth)),
                (aux_ref, aux_all_ref.at[ring.index]),
            )
        )
    ]
    quarter = cut.maps // 4
    half = cut.shared // 2
    rows = lambda number: pl.ds(number * quarter, quarter)

    def shared(which, way):
        return pl.ds(pl.multiple_of(cut.maps + which * cut.shared + way * half, 16), half)

    def piece(rows):
        return share_ref.at[rows], lambda index: block_at(w_ref, index, rows, depth)

    ways = (
        [
            piece(rows(0)),
            piece(rows(1)),
            piece(shared(core, 0)),
            (aux_ref, lambda index: aux_all_ref.at[index]),
        ],
        [piece(rows(2)), piece(rows(3)), piece(shared(core, 1))],
    )

    def over_core(step, way, which):
        here = block_at(w_ref, ring.at((2 * way - 1) * step), shared(which, way), depth)
        return remote(
            here, here, core_send.at[step - 1, way], core_recv.at[step - 1, way], pair.peers[1]
        )

    def hook(step, way, piece):
        if piece == 2:
            over_core(step, way, core).start()

    gather = Gather(ring, ways, send, recv, hook)
    gather.start()
    tokens = Share(pair, 1, tokens_ref, tokens_all_ref, token_sems)
    branch = Share(pair, 1, branch_ref, branch_all_ref, branch_sems)
    tokens.start(0)
    branch.start(0)
    for keep in keeps:
        keep.start()
    gather.run(2, 4)
    tokens.pass_on(0)
    gather.advance(4)
    branch.pass_on(0)
    gather.advance(5)
    tokens.finish()
    for keep in keeps:
        keep.wait()
    if inside:
        length = tokens_ref.shape[0]
        chunk = cut.width // 7

        def scale(number, carry):
            values = tokens_all_ref[number].astype(F32)
            rows = pl.ds(pl.multiple_of(number * length, length), length)
            scale_ref[rows] = jnp.broadcast_to(norm_scale(values), (length, LANES))
            return carry

        lax.fori_loop(0, 4, scale, 0)

    def add(offset, fresh=False, last=False):
        index = ring.at(offset)
        if not fresh:
            over_core(offset, 1, 1 - core).wait_recv()
            over_core(shards - offset, 0, 1 - core).wait_recv()
        lanes = pl.ds(pl.multiple_of(index * depth, LANES), depth)
        gain = aux_all_ref[index, 0:1, :].astype(F32)

        def body(number, carry):
            rows = pl.ds(pl.multiple_of(number * length, length), length)
            left = tokens_all_ref[number, :, lanes].astype(F32) * scale_ref[rows, 0:1] * gain
            left = left.astype(BF16)
            normed_ref[rows, lanes] = left
            for at in range(0, cut.width, chunk):
                out = slice(at, at + chunk)
                total = dot_nt(left, w_ref[out, lanes])
                if not fresh:
                    total = sum_ref[rows, out] + total
                if not last:
                    sum_ref[rows, out] = total
                    continue
                proj_ref[rows, out] = total.astype(BF16)
                if at <= cut.step < at + chunk:
                    steps_ref[rows] = total[:, cut.step - at : cut.step - at + LANES]
            return carry

        lax.fori_loop(0, 4, body, 0)
        store(offset).start()

    def store(offset):
        lanes = pl.ds(pl.multiple_of(ring.at(offset) * depth, LANES), depth)
        return pltpu.make_async_copy(w_ref.at[:, lanes], w_out_ref.at[:, lanes], w_sem.at[offset])

    done = {0}
    if inside:
        add(0, True)

    def add_landed(step):
        for offset in range(1, shards):
            if inside and offset not in done and max(offset, shards - offset) <= step:
                done.add(offset)
                add(offset, False, len(done) == shards)

    add_landed(4)
    gather.advance(6)
    add_landed(5)
    gather.run(7, shards)
    add_landed(shards - 2)
    gather.finish()
    add_landed(shards - 1)

    def rest(step, carry):
        for way in range(2):
            if not inside:
                over_core(step, way, 1 - core).wait_recv()
            over_core(step, way, core).wait_send()
        return carry

    lax.fori_loop(1, shards, rest, 0)
    branch.finish()
    if inside:
        for offset in range(shards):
            store(offset).wait()


def share_sems(chunks):
    return [
        pltpu.SemaphoreType.DMA((3, chunks)),
        pltpu.SemaphoreType.DMA((3, chunks)),
        pltpu.SemaphoreType.DMA((chunks,)),
    ]


def gather_in_call(shards, cut, in_t, query, key, value, aux, tokens, cot, live):
    depth = in_t.shape[1]
    length, width = tokens.shape
    inside = depth % LANES == 0
    hbm = pl.BlockSpec(memory_space=pl.ANY)
    vmem = pl.BlockSpec(memory_space=pltpu.VMEM)
    out_shape = [
        jax.ShapeDtypeStruct((shards,) + aux.shape, BF16),
        jax.ShapeDtypeStruct((4, length, width), BF16),
    ]
    scratch = [
        pltpu.VMEM((cut.width, depth), BF16),
        pltpu.VMEM((depth, cut.qwidth + 2 * HEAD_WIDTH), BF16),
        pltpu.VMEM((HEADS, depth), BF16),
        pltpu.VMEM((length, width), BF16),
        pltpu.SemaphoreType.DMA((9,)),
        *ring_sems(shards, 4),
        pltpu.SemaphoreType.DMA((shards - 1, 2)),
        pltpu.SemaphoreType.DMA((shards - 1, 2)),
        *share_sems(1),
        *share_sems(1),
    ]
    if inside:
        rows = 4 * length
        out_shape = [jax.ShapeDtypeStruct((cut.width, width), BF16)] + out_shape
        out_shape += [
            jax.ShapeDtypeStruct((rows, width), BF16),
            jax.ShapeDtypeStruct((rows, cut.width), BF16),
            jax.ShapeDtypeStruct((rows, LANES), F32),
        ]
        out_specs = [hbm, vmem, hbm] + [vmem] * 3
        scratch += [
            pltpu.VMEM((rows, cut.width), F32),
            pltpu.VMEM((rows, LANES), F32),
            pltpu.SemaphoreType.DMA((shards,)),
            pltpu.VMEM((cut.width, width), BF16),
            pltpu.VMEM((4, length, width), BF16),
        ]
    else:
        out_shape = [jax.ShapeDtypeStruct((shards, cut.width, depth), BF16)] + out_shape
        out_shape += [jax.ShapeDtypeStruct((4, length, width), BF16)]
        out_specs = [hbm] * 4
    return pl.pallas_call(
        functools.partial(gather_in, shards, cut, inside),
        out_shape=out_shape,
        in_specs=[hbm] * 6 + [vmem] * 2,
        out_specs=out_specs,
        scratch_shapes=scratch,
        compiler_params=pltpu.CompilerParams(
            collective_id=0, has_side_effects=True, vmem_limit_bytes=56 * MIB
        ),
        name="gather_in",
    )(in_t, query, key, value, aux, tokens, cot, live)


def gather_rows(
    shards,
    cut,
    length,
    heads_ref,
    down_ref,
    proj_ref,
    step_ref,
    conv_ref,
    head_ref,
    chan_ref,
    cos_ref,
    sin_ref,
    heads_all_ref,
    down_all_ref,
    out_ref,
    act_ref,
    pack_sem,
    send,
    recv,
):
    ring, pair = Ring(shards), Pair()
    half = down_ref.shape[0] // 2
    rows = lambda number: pl.ds(number * half, half)
    down_way = [
        (
            down_ref.at[rows(number)],
            lambda index, number=number: down_all_ref.at[index, rows(number)],
        )
        for number in range(2)
    ]
    if len(heads_all_ref.shape) == 2:
        mamba = cut.inner // shards
        attn = heads_ref.shape[0] - mamba

        def mamba_place(index):
            return heads_all_ref.at[pl.ds(pl.multiple_of(index * mamba, 16), mamba)]

        def attn_place(index):
            start = pl.multiple_of(cut.inner + index * attn, 16)
            return heads_all_ref.at[pl.ds(start, attn)]

        heads_way = [
            (heads_ref.at[pl.ds(0, mamba)], mamba_place),
            (heads_ref.at[pl.ds(mamba, attn)], attn_place),
        ]
    else:
        heads_way = [
            (
                heads_ref.at[rows(number)],
                lambda index, number=number: heads_all_ref.at[index, rows(number)],
            )
            for number in range(2)
        ]
    ways = (heads_way, down_way)
    packs = [
        pltpu.make_async_copy(own, place(ring.index), pack_sem.at[2 * way + number])
        for way in range(2)
        for number, (own, place) in enumerate(ways[way])
    ]
    for pack in packs:
        pack.start()
    greet(ring, pair)
    gather = Gather(ring, ways, send, recv)
    gather.start()
    count = proj_ref.shape[0] // length

    def body(number, carry):
        rows = pl.ds(pl.multiple_of(number * length, length), length)
        mixer_forward(
            cut,
            proj_ref.at[rows],
            step_ref.at[rows],
            conv_ref,
            head_ref,
            chan_ref,
            cos_ref,
            sin_ref,
            out_ref.at[rows],
            act_ref,
        )
        gather.advance(number + 2)
        return carry

    lax.fori_loop(0, count, body, 0)
    gather.run(count + 2, shards)
    gather.finish()
    for pack in packs:
        pack.wait()


def gather_rows_call(
    shards, cut, length, ordered, heads, down, proj, steps, conv, head, chan, cosine, sine
):
    rows = proj.shape[0]
    tall, width = heads.shape
    hbm = pl.BlockSpec(memory_space=pl.ANY)
    vmem = pl.BlockSpec(memory_space=pltpu.VMEM)
    return pl.pallas_call(
        functools.partial(gather_rows, shards, cut, length),
        out_shape=[
            jax.ShapeDtypeStruct(
                (shards * tall, width) if ordered else (shards, tall, width), BF16
            ),
            jax.ShapeDtypeStruct((shards,) + down.shape, BF16),
            jax.ShapeDtypeStruct((rows, cut.inner + cut.qwidth), BF16),
        ],
        in_specs=[vmem] * 9,
        out_specs=[hbm] * 2 + [vmem],
        scratch_shapes=[
            pltpu.VMEM((length, cut.conv), F32),
            pltpu.SemaphoreType.DMA((4,)),
        ]
        + ring_sems(shards, 2),
        compiler_params=pltpu.CompilerParams(
            collective_id=1, has_side_effects=True, vmem_limit_bytes=48 * MIB
        ),
        name="gather_rows",
    )(heads, down, proj, steps, conv, head, chan, cosine, sine)


class Exchange:
    def __init__(self, pair, chunks, part_ref, core_ref, cross_ref, came_ref, sems):
        self.pair, self.chunks = pair, chunks
        self.part, self.core, self.cross, self.came = part_ref, core_ref, cross_ref, came_ref
        self.send, self.recv = sems
        self.tall = part_ref.shape[1] // chunks

    def rows(self, chunk):
        return pl.ds(chunk * self.tall, self.tall)

    def over_core(self, chunk, which):
        return remote(
            self.part.at[2 + which, self.rows(chunk)],
            self.core.at[which, self.rows(chunk)],
            self.send.at[0, which, chunk],
            self.recv.at[0, which, chunk],
            self.pair.peers[1],
        )

    def over_x(self, chunk):
        return remote(
            self.cross.at[self.rows(chunk)],
            self.came.at[self.rows(chunk)],
            self.send.at[1, 0, chunk],
            self.recv.at[1, 0, chunk],
            self.pair.peers[0],
        )

    def start_one(self, which):
        for chunk in range(self.chunks):
            self.over_core(chunk, which).start()

    def start(self):
        self.start_one(1)
        self.start_one(0)

    def middle(self, chunk):
        self.over_core(chunk, 1).wait_recv()
        rows = self.rows(chunk)
        total = self.part[1, rows].astype(F32) + self.core[1, rows].astype(F32)
        self.cross[rows] = total.astype(BF16)
        self.over_x(chunk).start()

    def sum(self, chunk):
        self.over_core(chunk, 0).wait_recv()
        self.over_x(chunk).wait_recv()
        rows = self.rows(chunk)
        return (
            self.part[0, rows].astype(F32)
            + self.core[0, rows].astype(F32)
            + self.came[rows].astype(F32)
        )

    def finish(self):
        for chunk in range(self.chunks):
            for which in range(2):
                self.over_core(chunk, which).wait_send()
            self.over_x(chunk).wait_send()


class Share:
    def __init__(self, pair, chunks, own_ref, all_ref, sems):
        self.pair, self.chunks, self.own, self.all = pair, chunks, own_ref, all_ref
        self.send, self.recv, self.local = sems
        self.tall = own_ref.shape[0] // chunks

    def rows(self, chunk):
        return pl.ds(chunk * self.tall, self.tall)

    def direct(self, chunk, which):
        return remote(
            self.own.at[self.rows(chunk)],
            self.all.at[1 + which, self.rows(chunk)],
            self.send.at[which, chunk],
            self.recv.at[which, chunk],
            self.pair.peers[which],
        )

    def onward(self, chunk):
        return remote(
            self.all.at[1, self.rows(chunk)],
            self.all.at[3, self.rows(chunk)],
            self.send.at[2, chunk],
            self.recv.at[2, chunk],
            self.pair.peers[1],
        )

    def keep(self, chunk):
        return pltpu.make_async_copy(
            self.own.at[self.rows(chunk)], self.all.at[0, self.rows(chunk)], self.local.at[chunk]
        )

    def start(self, chunk):
        self.direct(chunk, 0).start()
        self.direct(chunk, 1).start()
        self.keep(chunk).start()

    def pass_on(self, chunk):
        self.direct(chunk, 0).wait_recv()
        self.onward(chunk).start()

    def finish(self):
        for chunk in range(self.chunks):
            self.direct(chunk, 0).wait_send()
            self.direct(chunk, 1).wait()
            self.onward(chunk).wait()
            self.keep(chunk).wait()


CHUNKS = 2


def exchange_scratch(length, width):
    return [
        pltpu.VMEM((2, length, width), BF16),
        pltpu.VMEM((length, width), BF16),
        pltpu.VMEM((length, width), BF16),
        pltpu.SemaphoreType.DMA((2, 2, CHUNKS)),
        pltpu.SemaphoreType.DMA((2, 2, CHUNKS)),
    ]


class Scatter:
    def __init__(self, ring, pieces, term, first_ref, slots_ref, send, recv, groups=1):
        self.ring, self.pieces, self.groups, self.term = ring, pieces, groups, term
        self.first, self.slots, self.send, self.recv = first_ref, slots_ref, send, recv
        self.half = slots_ref.shape[2]
        self.tall = self.half // pieces

    def each(self, group):
        size = self.pieces // self.groups
        for piece in range(group * size, (group + 1) * size):
            for way in range(2):
                yield way, piece

    def rows(self, way, piece):
        return pl.ds(way * self.half + piece * self.tall, self.tall)

    def local(self, piece):
        return pl.ds(piece * self.tall, self.tall)

    def due(self, step, way, piece):
        return self.term(self.ring.at((2 * way - 1) * step), self.rows(way, piece))

    def copy(self, step, way, piece, first=False):
        src = self.first.at[way] if first else self.slots.at[step - 2, way]
        return remote(
            src.at[self.local(piece)],
            self.slots.at[step - 1, way, self.local(piece)],
            self.send.at[step - 1, way, piece],
            self.recv.at[step - 1, way, piece],
            self.ring.peer(way),
        )

    def landed(self, step, way, piece):
        here = self.slots.at[step - 1, way, self.local(piece)]
        return remote(
            here,
            here,
            self.send.at[step - 1, way, piece],
            self.recv.at[step - 1, way, piece],
            self.ring.peer(way),
        )

    def start(self, group=0):
        for way, piece in self.each(group):
            self.first[way, self.local(piece)] = self.due(1, way, piece).astype(BF16)
            self.copy(1, way, piece, True).start()

    def total(self, step, way, piece):
        term = self.due(step, way, piece)
        self.landed(step - 1, way, piece).wait_recv()
        return self.slots[step - 2, way, self.local(piece)].astype(F32) + term

    def advance(self, step, group=0):
        for way, piece in self.each(group):
            total = self.total(step, way, piece)
            self.slots[step - 2, way, self.local(piece)] = total.astype(BF16)
            self.copy(step, way, piece).start()

    def run(self, first, stop, group=0):
        def body(step, carry):
            self.advance(step, group)
            return carry

        lax.fori_loop(first, stop, body, 0)

    def result(self, own_ref, share=None, group=0):
        for way, piece in self.each(group):
            total = self.total(self.ring.shards, way, piece)
            own_ref[self.rows(way, piece)] = total.astype(BF16)
            if share is not None:
                share.start(way * self.pieces + piece)

    def chunks(self, group):
        return [way * self.pieces + piece for way, piece in self.each(group)]

    def finish(self):
        for group in range(self.groups):
            for way, piece in self.each(group):
                self.copy(1, way, piece, True).wait_send()

        def body(step, carry):
            for group in range(self.groups):
                for way, piece in self.each(group):
                    self.copy(step, way, piece).wait_send()
            return carry

        lax.fori_loop(2, self.ring.shards, body, 0)


def stored(ref):
    return lambda index, rows: ref[index, rows].astype(F32)


def pieces_of(rows):
    return 2 if rows // 2 % 32 == 0 else 1


def scatter_scratch(shards, rows, width, pieces=None):
    return [
        pltpu.VMEM((2, rows // 2, width), BF16),
        pltpu.VMEM((shards - 1, 2, rows // 2, width), BF16),
    ] + ring_sems(shards, pieces or pieces_of(rows))


def share_scratch(rows, width, chunks):
    return [
        pltpu.VMEM((rows, width), BF16),
        pltpu.SemaphoreType.DMA((3, chunks)),
        pltpu.SemaphoreType.DMA((3, chunks)),
        pltpu.SemaphoreType.DMA((chunks,)),
    ]


def gather_mlp(shards, inside, count, *refs):
    refs = list(refs)
    take = lambda number: [refs.pop(0) for _ in range(number)]
    source_refs = take(count)
    heads_ref, w_out_ref, tokens_ref, live_ref, gain_ref = take(5)
    all_ref, normed_ref, mixed_ref = take(3)
    if inside:
        (sum_ref,) = take(1)
    core_ref, cross_ref, came_ref, ex_send, ex_recv = take(5)
    own_ref, sh_send, sh_recv, sh_local = take(4)
    part_ref, share_ref, pack_sem, send, recv = take(5)

    ring, pair = Ring(shards), Pair()
    depth, wide = share_ref.shape
    if count == 1:
        packs = [pltpu.make_async_copy(source_refs[0], share_ref, pack_sem.at[0])]
    else:
        units = wide // (2 * shards)
        packs = [
            pltpu.make_async_copy(
                ref.at[:, pl.ds(pl.multiple_of((shard * 4 + pair.rep) * units, LANES), units)],
                share_ref.at[:, pl.ds((which * shards + shard) * units, units)],
                pack_sem.at[which * shards + shard],
            )
            for which, ref in enumerate(source_refs)
            for shard in range(shards)
        ]
    for pack in packs:
        pack.start()
    greet(ring, pair)
    for pack in packs:
        pack.wait()
    keep = pltpu.make_async_copy(share_ref, all_ref.at[ring.index], pack_sem.at[0])
    keep.start()
    quarter = depth // 4
    rows = lambda number: pl.ds(number * quarter, quarter)
    piece = lambda number: (
        share_ref.at[rows(number)],
        lambda index: all_ref.at[index, rows(number)],
    )
    gather = Gather(ring, ([piece(0), piece(1)], [piece(2), piece(3)]), send, recv)
    exchange = Exchange(
        pair, CHUNKS, part_ref, core_ref, cross_ref, came_ref, (ex_send, ex_recv)
    )
    share = Share(pair, CHUNKS, own_ref, normed_ref, (sh_send, sh_recv, sh_local))
    length = part_ref.shape[1]

    def partial(number):
        left = heads_ref[pl.ds(number * length, length)]
        for lane in range(0, part_ref.shape[2], WIDE):
            lanes = slice(lane, lane + WIDE)
            part_ref[number, :, lanes] = dot(left, w_out_ref[:, lanes]).astype(BF16)

    def middle(chunk):
        rows = exchange.rows(chunk)
        branch = exchange.sum(chunk)
        mixed = tokens_ref[rows].astype(F32) + live_ref[rows, 0:1] * branch
        mixed_ref[rows] = mixed
        own_ref[rows] = (mixed * norm_scale(mixed) * gain_ref[0:1]).astype(BF16)
        share.start(chunk)

    def add(index, fresh=False):
        if not inside:
            return
        deep = pl.ds(pl.multiple_of(index * depth, LANES), depth)

        def body(number, carry):
            left = normed_ref[number, :, deep]
            rows = pl.ds(pl.multiple_of(number * length, length), length)
            for lane in range(0, wide, WIDE):
                lanes = slice(lane, lane + WIDE)
                term = dot(left, all_ref[index, :, lanes])
                sum_ref[rows, lanes] = term if fresh else sum_ref[rows, lanes] + term
            return carry

        lax.fori_loop(0, 4, body, 0)

    gather.start()
    for number in (3, 2, 1, 0):
        partial(number)
        if number > 1:
            exchange.start_one(number - 2)
    exchange.middle(0)
    exchange.middle(1)
    gather.advance(2)
    middle(0)
    gather.advance(3)
    middle(1)
    gather.advance(4)
    share.pass_on(0)
    gather.advance(5)
    share.pass_on(1)
    gather.advance(6)
    share.finish()
    keep.wait()
    half_way = shards // 2
    add(ring.index, True)
    if half_way < 6:
        add(ring.at(half_way))
    gather.run(7, shards)
    if half_way >= 6:
        add(ring.at(half_way))
    if inside:

        def body(far, carry):
            add(ring.at(far))
            add(ring.at(-far))
            return carry

        lax.fori_loop(2, half_way, body, 0)
    gather.finish()
    add(ring.at(1))
    add(ring.at(-1))
    exchange.finish()


def gather_mlp_call(shards, inside, sources, wide, heads, w_out, tokens, live, gain):
    length, width = tokens.shape
    depth = sources[0].shape[0]
    hbm = pl.BlockSpec(memory_space=pl.ANY)
    vmem = pl.BlockSpec(memory_space=pltpu.VMEM)
    rows = heads.shape[0]
    return pl.pallas_call(
        functools.partial(gather_mlp, shards, inside, len(sources)),
        out_shape=[
            jax.ShapeDtypeStruct((shards, depth, wide), BF16),
            jax.ShapeDtypeStruct((4, length, width), BF16),
            jax.ShapeDtypeStruct((length, width), F32),
        ]
        + [jax.ShapeDtypeStruct((rows, wide), F32)] * inside,
        in_specs=[hbm] * len(sources) + [vmem] * 5,
        out_specs=[vmem] * (3 + inside),
        scratch_shapes=exchange_scratch(length, width)
        + share_scratch(length, width, CHUNKS)
        + [
            pltpu.VMEM((4, length, width), BF16),
            pltpu.VMEM((depth, wide), BF16),
            pltpu.SemaphoreType.DMA((2 * shards,)),
        ]
        + ring_sems(shards, 2),
        compiler_params=pltpu.CompilerParams(
            collective_id=2, has_side_effects=True, vmem_limit_bytes=56 * MIB
        ),
        name="gather_mlp",
    )(*sources, heads, w_out, tokens, live, gain)


TILE = 256
WIDE = 512


def product_tn(left_ref, right_ref, out_ref, number):
    rows = pl.ds(pl.multiple_of(number * TILE, TILE), TILE)
    left = left_ref[:, rows].T
    for lane in range(0, out_ref.shape[1], WIDE):
        lanes = slice(lane, lane + WIDE)
        out_ref[rows, lanes] = dot(left, right_ref[:, lanes]).astype(out_ref.dtype)


def product(left_ref, right_ref, out_ref, number):
    rows = pl.ds(pl.multiple_of(number * TILE, TILE), TILE)
    for lane in range(0, out_ref.shape[1], WIDE):
        lanes = slice(lane, lane + WIDE)
        out_ref[rows, lanes] = dot(left_ref[rows], right_ref[:, lanes]).astype(out_ref.dtype)


def mlp_back(gate_up_ref, branch_ref, w_down_ref, w_mlp_ref, active_ref, d_ref, part_ref):
    half = active_ref.shape[1]
    for lane in range(0, half, WIDE):
        gates, ups = slice(lane, lane + WIDE), slice(half + lane, half + lane + WIDE)
        d_active = dot_nt(branch_ref[...], w_down_ref[gates])
        gate, up = gate_up_ref[:, gates], gate_up_ref[:, ups]
        sig = sigmoid(gate)
        active = gate * sig
        active_ref[:, gates] = (active * up).astype(BF16)
        d_ref[:, gates] = (d_active * up * silu_slope(gate, sig)).astype(BF16)
        d_ref[:, ups] = (d_active * active).astype(BF16)
    for lane in range(0, part_ref.shape[1], WIDE):
        lanes = slice(lane, lane + WIDE)
        part_ref[:, lanes] = dot_nt(d_ref[...], w_mlp_ref[lanes]).astype(BF16)


def mlp_back_call(gate_up, branch, w_down, w_mlp):
    rows, wide = gate_up.shape
    half, width = w_down.shape
    tall = 2 * TILE
    tile = lambda lanes: pl.BlockSpec((tall, lanes), lambda i: (i, 0))
    whole = lambda shape: pl.BlockSpec(shape, lambda i: (0, 0))
    return pl.pallas_call(
        mlp_back,
        grid=(rows // tall,),
        out_shape=[
            jax.ShapeDtypeStruct((rows, half), BF16),
            jax.ShapeDtypeStruct((rows, wide), BF16),
            jax.ShapeDtypeStruct((rows, width), BF16),
        ],
        in_specs=[tile(wide), tile(width), whole(w_down.shape), whole(w_mlp.shape)],
        out_specs=[tile(half), tile(wide), tile(width)],
        compiler_params=pltpu.CompilerParams(vmem_limit_bytes=56 * MIB),
        name="mlp_back",
    )(gate_up, branch, w_down, w_mlp)


def scatter_down(
    shards,
    part_ref,
    branch_two_ref,
    normed_ref,
    d_mlp_ref,
    active_ref,
    w_down_ref,
    mixed_ref,
    cot_ref,
    live_ref,
    gain_ref,
    branch_ref,
    down_own_ref,
    mlp_ref,
    ffn_ref,
    d_mixed_ref,
    gain_sum_ref,
    core_ref,
    cross_ref,
    came_ref,
    ex_send,
    ex_recv,
    own_ref,
    sh_send,
    sh_recv,
    sh_local,
    first_ref,
    slots_ref,
    send,
    recv,
    down_ref,
):
    ring, pair = Ring(shards), Pair()
    greet(ring, pair)
    units = slots_ref.shape[2] * 2

    def down_term(index, rows):
        start = pl.multiple_of(index * units + rows.start, 16)
        return down_ref[pl.ds(start, rows.size)].astype(F32)

    scatter = Scatter(ring, pieces_of(units), down_term, first_ref, slots_ref, send, recv)
    exchange = Exchange(
        pair, CHUNKS, part_ref, core_ref, cross_ref, came_ref, (ex_send, ex_recv)
    )
    share = Share(pair, CHUNKS, own_ref, branch_ref, (sh_send, sh_recv, sh_local))
    gain_sum_ref[...] = jnp.zeros_like(gain_sum_ref)

    def middle(chunk):
        rows = exchange.rows(chunk)
        grad = exchange.sum(chunk)
        values = mixed_ref[rows]
        d_values, gain_sum = norm_back(values, norm_scale(values), gain_ref[0:1], grad)
        gain_sum_ref[0:1] += gain_sum
        d_mixed = cot_ref[rows].astype(F32) + d_values
        d_mixed_ref[rows] = d_mixed
        own_ref[rows] = (live_ref[rows, 0:1] * d_mixed).astype(BF16)
        share.start(chunk)

    def work(first, stop):
        def body(number, carry):
            product_tn(normed_ref, d_mlp_ref, mlp_ref, number)
            return carry

        lax.fori_loop(first, stop, body, 0)

    tiles = mlp_ref.shape[0] // TILE
    exchange.start()

    def down(number, carry):
        product_tn(active_ref, branch_two_ref, down_ref, number)
        return carry

    lax.fori_loop(0, down_ref.shape[0] // TILE, down, 0)
    scatter.start()
    exchange.middle(0)
    exchange.middle(1)
    scatter.advance(2)
    work(0, 3)
    scatter.advance(3)
    work(3, 5)
    middle(0)
    scatter.advance(4)
    work(5, 6)
    scatter.advance(5)
    middle(1)
    scatter.advance(6)
    work(6, tiles)
    scatter.run(7, shards)

    def rest(number, carry):
        product(active_ref, w_down_ref, ffn_ref, number)
        return carry

    lax.fori_loop(0, ffn_ref.shape[0] // TILE, rest, 0)
    scatter.result(down_own_ref)
    share.pass_on(0)
    share.pass_on(1)
    scatter.finish()
    exchange.finish()
    share.finish()


def scatter_down_call(
    shards, part, branch_two, normed, d_mlp, active, w_down, mixed, cot, live, gain
):
    length, width = mixed.shape
    hbm = pl.BlockSpec(memory_space=pl.ANY)
    vmem = pl.BlockSpec(memory_space=pltpu.VMEM)
    units = active.shape[1] // shards
    return pl.pallas_call(
        functools.partial(scatter_down, shards),
        out_shape=[
            jax.ShapeDtypeStruct((4, length, width), BF16),
            jax.ShapeDtypeStruct((units, width), BF16),
            jax.ShapeDtypeStruct((normed.shape[1], d_mlp.shape[1]), BF16),
            jax.ShapeDtypeStruct((4 * length, width), BF16),
            jax.ShapeDtypeStruct((length, width), F32),
            jax.ShapeDtypeStruct((8, width), F32),
        ],
        in_specs=[vmem] * 10,
        out_specs=[hbm] + [vmem] * 5,
        scratch_shapes=exchange_scratch(length, width)
        + share_scratch(length, width, CHUNKS)
        + scatter_scratch(shards, units, width)
        + [pltpu.VMEM((units * shards, width), BF16)],
        compiler_params=pltpu.CompilerParams(
            collective_id=3, has_side_effects=True, vmem_limit_bytes=60 * MIB
        ),
        name="scatter_down",
    )(part, branch_two, normed, d_mlp, active, w_down, mixed, cot, live, gain)


def scatter_mlp(
    shards,
    cut,
    length,
    mlp_ref,
    out_ref,
    proj_ref,
    step_ref,
    grad_ref,
    conv_ref,
    head_ref,
    chan_ref,
    cos_ref,
    sin_ref,
    down_ref,
    ffn_ref,
    down_all_ref,
    ffn_came_ref,
    mlp_own_ref,
    out_own_ref,
    d_ref,
    d_t_ref,
    conv_sum_ref,
    head_sum_ref,
    chan_sum_ref,
    act_ref,
    d_act_ref,
    d_pair_ref,
    col_ref,
    first_ref,
    slots_ref,
    send,
    recv,
    out_first_ref,
    out_slots_ref,
    out_send,
    out_recv,
    sh_send,
    sh_recv,
    sh_local,
    ffn_send,
    ffn_recv,
    shared_ref,
    shared_came_ref,
    add_sem,
):
    ring, pair = Ring(shards), Pair()
    greet(ring, pair, pair.corner)
    share = Share(pair, 1, down_ref, down_all_ref, (sh_send, sh_recv, sh_local))
    ffn = [
        remote(
            ffn_ref.at[1 + which],
            ffn_came_ref.at[which],
            ffn_send.at[which],
            ffn_recv.at[which],
            peer,
        )
        for which, peer in enumerate(pair.peers + (pair.corner,))
    ]
    mlp = Scatter(
        ring, pieces_of(mlp_ref.shape[1]), stored(mlp_ref), first_ref, slots_ref, send, recv
    )
    tall = out_slots_ref.shape[2] * 2
    mamba = cut.inner // shards

    def out_rows(index, rows):
        if rows.start < mamba:
            start = index * mamba + rows.start
        else:
            start = cut.inner + index * (tall - mamba) + rows.start - mamba
        return out_ref[pl.ds(pl.multiple_of(start, 16), rows.size)].astype(F32)

    out = Scatter(
        ring,
        pieces_of(tall),
        stored(out_ref) if len(out_ref.shape) == 3 else out_rows,
        out_first_ref,
        out_slots_ref,
        out_send,
        out_recv,
    )
    mlp.start()
    out.start()
    share.start(0)
    for copy in ffn:
        copy.start()
    for ref in (conv_sum_ref, head_sum_ref, chan_sum_ref):
        ref[...] = jnp.zeros_like(ref)
    count = proj_ref.shape[0] // length

    def body(number, carry):
        rows = pl.ds(pl.multiple_of(number * length, length), length)
        mixer_backward(
            cut,
            proj_ref.at[rows],
            step_ref.at[rows],
            grad_ref.at[rows],
            conv_ref,
            head_ref,
            chan_ref,
            cos_ref,
            sin_ref,
            d_ref.at[rows],
            conv_sum_ref,
            head_sum_ref,
            chan_sum_ref,
            act_ref,
            d_act_ref,
            d_pair_ref,
            col_ref,
        )
        mlp.advance(number + 2)
        out.advance(number + 2)
        half = LANES // 2
        for lane in range(0, cut.width, LANES):
            turned = d_ref[rows, lane : lane + LANES].T
            if lane >= cut.maps:
                shared_ref[lane - cut.maps : lane - cut.maps + LANES, rows] = turned
                continue
            for part in range(2):
                to = cut.ring_row(lane + part * half)
                d_t_ref[to : to + half, rows] = turned[part * half : (part + 1) * half]
        return carry

    lax.fori_loop(0, count, body, 0)
    core = pair.rep % 2
    of_core = lambda which: pl.multiple_of(which * cut.shared, 16)
    add = remote(
        shared_ref.at[pl.ds(of_core(1 - core), cut.shared)],
        shared_came_ref,
        add_sem.at[0],
        add_sem.at[1],
        pair.peers[1],
    )
    add.start()
    share.pass_on(0)
    mlp.advance(count + 2)
    out.advance(count + 2)
    add.wait()
    half = cut.shared // 2
    for way in range(2):
        rows = pl.ds(pl.multiple_of(of_core(core) + way * half, 16), half)
        to = way * cut.way + cut.maps // 2
        middle = 2 * length
        for here, there in ((0, middle), (middle, 0)):
            total = shared_ref[rows, here : here + middle].astype(F32)
            total = total + shared_came_ref[
                way * half : (way + 1) * half, there : there + middle
            ].astype(F32)
            d_t_ref[to : to + half, here : here + middle] = total.astype(BF16)

    def rest(step, carry):
        mlp.advance(step)
        out.advance(step)
        return carry

    lax.fori_loop(count + 3, shards, rest, 0)
    mlp.result(mlp_own_ref)
    out.result(out_own_ref)
    mlp.finish()
    out.finish()
    share.finish()
    for copy in ffn:
        copy.wait()


def scatter_mlp_call(
    shards, cut, length, mlp, out, proj, steps, grad, conv, head, chan, cosine, sine, down, ffn
):
    hbm = pl.BlockSpec(memory_space=pl.ANY)
    rows = proj.shape[0]
    vmem = pl.BlockSpec(memory_space=pltpu.VMEM)
    depth, wide = mlp.shape[1:]
    width = out.shape[-1]
    tall = out.size // width // shards
    return pl.pallas_call(
        functools.partial(scatter_mlp, shards, cut, length),
        out_shape=[
            jax.ShapeDtypeStruct((4,) + down.shape, BF16),
            jax.ShapeDtypeStruct((3, length, width), BF16),
            jax.ShapeDtypeStruct((depth, wide), BF16),
            jax.ShapeDtypeStruct((tall, width), BF16),
            jax.ShapeDtypeStruct((rows, cut.width), BF16),
            jax.ShapeDtypeStruct((2 * cut.way, rows), BF16),
            jax.ShapeDtypeStruct(conv.shape, F32),
            jax.ShapeDtypeStruct(head.shape, F32),
            jax.ShapeDtypeStruct(chan.shape, F32),
        ],
        in_specs=[vmem] * 11 + [hbm],
        out_specs=[hbm] * 2 + [vmem] * 7,
        scratch_shapes=[
            pltpu.VMEM((length, cut.conv), F32),
            pltpu.VMEM((length, cut.conv), F32),
            pltpu.VMEM((length, length), F32),
            pltpu.VMEM((LANES, length), F32),
        ]
        + scatter_scratch(shards, depth, wide)
        + scatter_scratch(shards, tall, width)
        + share_sems(1)
        + [pltpu.SemaphoreType.DMA((3,))] * 2
        + [
            pltpu.VMEM((2 * cut.shared, rows), BF16),
            pltpu.VMEM((cut.shared, rows), BF16),
            pltpu.SemaphoreType.DMA((2,)),
        ],
        compiler_params=pltpu.CompilerParams(
            collective_id=4, has_side_effects=True, vmem_limit_bytes=60 * MIB
        ),
        name="scatter_mlp",
    )(mlp, out, proj, steps, grad, conv, head, chan, cosine, sine, down, ffn)


GROUPS = 2
PIECES = 6


def scatter_in(shards, inside, *refs):
    refs = list(refs)
    take = lambda count: [refs.pop(0) for _ in range(count)]
    if inside:
        d_t_ref, normed_ref, d_hbm, w_hbm = take(4)
    else:
        in_ref, part_ref = take(2)
    small_ref, tokens_ref, d_mixed_ref, gain_ref, mlp_ref, out_ref = take(6)
    in_all_ref, small_all_ref, mlp_all_ref, out_all_ref, grad_ref = take(5)
    core_ref, cross_ref, came_ref, ex_send, ex_recv = take(5)
    in_scratch, small_scratch = take(4), take(4)
    own_ref, sh_send, sh_recv, sh_local = take(4)
    small_own_ref, sm_send, sm_recv, sm_local = take(4)
    mlp_sems, out_sems = take(3), take(3)
    move_ref, move_sem = take(2)
    if inside:
        d_ref, w_ref, part_ref, small_all, gain_sum_ref, load_sem = take(6)

    ring, pair = Ring(shards), Pair()
    if inside:
        loads = [
            pltpu.make_async_copy(src, dst, load_sem.at[number])
            for number, (src, dst) in enumerate(((d_hbm, d_ref), (w_hbm, w_ref)))
        ]
        for load in loads:
            load.start()
        depth = w_ref.shape[1] // shards

        def term(index, rows):
            lanes = pl.ds(pl.multiple_of(index * depth, LANES), depth)
            return dot(d_t_ref[rows], normed_ref[:, lanes])

        small_term = stored(small_all)
    else:
        term, small_term = stored(in_ref), stored(small_ref)
    group = shards // 4
    here, rep = ring.index, pair.rep
    to = (group * rep + here // 4, here % 4)
    by = (4 * (here % group) + rep, here // group)
    far = to[0] * 4 + to[1] - here * 4 - rep
    limit = (4 * shards) ** 2
    moves = (far * far + limit - 1) // limit
    peer = {"fsdp": to[0], "rep": to[1]}
    move = remote(out_ref, move_ref, move_sem.at[0], move_sem.at[1], peer)
    stay = pltpu.make_async_copy(out_ref, move_ref, move_sem.at[2])
    greet(ring, pair, maybe=(peer, {"fsdp": by[0], "rep": by[1]}), are=moves)

    @pl.when(moves == 1)
    def _():
        move.start()

    @pl.when(moves == 0)
    def _():
        stay.start()

    pieces = PIECES
    scatter = Scatter(ring, pieces, term, *in_scratch, groups=GROUPS)
    small = Scatter(ring, 1, small_term, *small_scratch)
    exchange = Exchange(
        pair, CHUNKS, part_ref, core_ref, cross_ref, came_ref, (ex_send, ex_recv)
    )
    share = Share(pair, 2 * pieces, own_ref, in_all_ref, (sh_send, sh_recv, sh_local))
    small_share = Share(pair, 2, small_own_ref, small_all_ref, (sm_send, sm_recv, sm_local))
    mlp_share = Share(pair, CHUNKS, mlp_ref, mlp_all_ref, mlp_sems)
    out_share = Share(pair, 1, move_ref, out_all_ref, out_sems)

    def middle(chunk):
        rows = exchange.rows(chunk)
        grad = exchange.sum(chunk)
        values = tokens_ref[rows].astype(F32)
        d_values, _ = norm_back(values, norm_scale(values), gain_ref[0:1], grad)
        grad_ref[rows] = (d_mixed_ref[rows] + d_values).astype(BF16)

    def partial(number):
        length = part_ref.shape[1]
        wide = 4 * LANES
        rows = pl.ds(number * length, length)

        def body(tile, carry):
            lanes = pl.ds(pl.multiple_of(tile * wide, wide), wide)
            grad = dot(d_ref[rows], w_ref[:, lanes])
            part_ref[number, :, lanes] = grad.astype(BF16)
            gain_sum_ref[0:1, lanes] += jnp.sum(
                grad * normed_ref[rows, lanes].astype(F32), axis=0, keepdims=True
            )
            return carry

        lax.fori_loop(0, w_ref.shape[1] // wide, body, 0)

    scatter.start(0)
    for chunk in range(CHUNKS):
        mlp_share.start(chunk)
    if inside:
        gain_sum_ref[...] = jnp.zeros_like(gain_sum_ref)
        for load in loads:
            load.wait()
    for number in range(4):
        if inside:
            partial(number)
        scatter.advance(number + 2, 0)
    if inside:
        small_all[...] = small_ref[...]
        gain_sum = gain_sum_ref[0:1] / gain_ref[0:1]
        for index in range(shards):
            for row in range(depth // LANES):
                at = index * depth + row * LANES
                small_all[index, row : row + 1] = gain_sum[:, at : at + LANES].astype(BF16)
    exchange.start()
    small.start()
    scatter.advance(6, 0)
    exchange.middle(0)
    small.advance(2)
    exchange.middle(1)

    @pl.when(moves == 1)
    def _():
        move.wait()

    @pl.when(moves == 0)
    def _():
        stay.wait()

    out_share.start(0)
    scatter.run(7, shards, 0)
    small.advance(3)
    scatter.start(1)
    scatter.result(own_ref, share, 0)
    for step in range(2, 6):
        scatter.advance(step, 1)
        small.advance(step + 2)
        if step in (3, 4):
            middle(step - 3)
    small.run(8, shards)
    for chunk in range(CHUNKS):
        mlp_share.pass_on(chunk)
    scatter.advance(6, 1)
    out_share.pass_on(0)
    small.result(small_own_ref, small_share)
    for chunk in scatter.chunks(0):
        share.pass_on(chunk)
    scatter.run(7, shards, 1)
    scatter.result(own_ref, share, 1)
    for chunk in range(2):
        small_share.pass_on(chunk)
    for chunk in scatter.chunks(1):
        share.pass_on(chunk)
    scatter.finish()
    small.finish()
    exchange.finish()
    share.finish()
    small_share.finish()
    mlp_share.finish()
    out_share.finish()


def scatter_in_call(shards, depth, inside, given, small, tokens, d_mixed, gain, mlp, out):
    length, width = tokens.shape
    hbm = pl.BlockSpec(memory_space=pl.ANY)
    vmem = pl.BlockSpec(memory_space=pltpu.VMEM)
    wide = given[0].shape[0] if inside else given[0].shape[-2]
    tall, lanes = small.shape[1:]
    extra = []
    if inside:
        extra = [
            pltpu.VMEM(given[2].shape, BF16),
            pltpu.VMEM(given[3].shape, BF16),
            pltpu.VMEM((4, length, width), BF16),
            pltpu.VMEM(small.shape, BF16),
            pltpu.VMEM((8, width), F32),
            pltpu.SemaphoreType.DMA((2,)),
        ]
    return pl.pallas_call(
        functools.partial(scatter_in, shards, inside),
        out_shape=[
            jax.ShapeDtypeStruct((4, wide, depth), BF16),
            jax.ShapeDtypeStruct((4, tall, lanes), BF16),
            jax.ShapeDtypeStruct((4,) + mlp.shape, BF16),
            jax.ShapeDtypeStruct((4,) + out.shape, BF16),
            jax.ShapeDtypeStruct((length, width), BF16),
        ],
        in_specs=([vmem] * 2 + [hbm] * 2 if inside else [vmem] * 2) + [vmem] * 6,
        out_specs=[hbm] * 4 + [vmem],
        scratch_shapes=exchange_scratch(length, width)
        + scatter_scratch(shards, wide, depth, PIECES)
        + scatter_scratch(shards, tall, lanes, 1)
        + share_scratch(wide, depth, 2 * PIECES)
        + share_scratch(tall, lanes, 2)
        + share_sems(CHUNKS)
        + share_sems(1)
        + [pltpu.VMEM(out.shape, BF16), pltpu.SemaphoreType.DMA((3,))]
        + extra,
        compiler_params=pltpu.CompilerParams(
            collective_id=5, has_side_effects=True, vmem_limit_bytes=60 * MIB
        ),
        name="scatter_in",
    )(*given, small, tokens, d_mixed, gain, mlp, out)


def columns(array, start, width):
    return lax.dynamic_slice_in_dim(array, start, width, axis=array.ndim - 1)


def norm_scale(values):
    return lax.rsqrt(jnp.mean(values * values, axis=-1, keepdims=True) + epsilon)


def norm_back(values, scale, gain, grad):
    inner = jnp.mean(gain * grad * values, axis=-1, keepdims=True)
    d_values = scale * gain * grad - values * (scale * scale * scale) * inner
    return d_values, jnp.sum(grad * values * scale, axis=0, keepdims=True)


def ring_at(position, shards):
    place = (position + 2 * shards) % shards
    back = place // (shards // 2)
    return (1 - back) * 2 * place + back * (2 * (shards - 1 - place) + 1)


def ring_place(index, shards):
    odd = index % 2
    return (1 - odd) * (index // 2) + odd * (shards - 1 - index // 2)


def after(value, *others):
    return lax.optimization_barrier((value,) + others)[0]


def rep_order(reps):
    order = [0]
    bit = reps // 2
    while bit:
        order = order + [member ^ bit for member in order]
        bit //= 2
    return order


def on_device(
    sizes,
    tokens,
    lengths,
    mixer_gain,
    in_proj,
    conv_weight,
    conv_bias,
    decay_log,
    step_bias,
    skip_gain,
    query_weight,
    key_weight,
    value_weight,
    mamba_out,
    attn_out,
    mlp_gain,
    gate_weight,
    up_weight,
    down_weight,
    cotangent,
):
    shards, reps = sizes
    cut = Cut(reps)
    rep = lax.axis_index("rep")
    fsdp = lax.axis_index("fsdp")
    place = ring_place(fsdp, shards)
    assert reps == 4
    length, width = tokens.shape
    depth = in_proj.shape[0]
    own = conv_weight.shape[1]
    channels = own * shards
    low = lambda v: v.astype(BF16)

    in_t = in_proj.T
    extra = 16
    aux = jnp.concatenate([mixer_gain, mlp_gain, conv_weight.reshape(-1), conv_bias], axis=0)
    aux_size = aux.shape[0]
    aux = jnp.pad(aux, (0, extra * 2 * LANES - aux_size)).reshape(extra, 2 * LANES)
    group = shards // reps
    pairs = [
        (g * reps + part, (reps * (g % group) + part) * reps + g // group)
        for g in range(shards)
        for part in range(reps)
    ]
    mamba_rows = mamba_out.shape[0] // reps
    attn_rows = attn_out.shape[0] // reps
    out_rows = mamba_rows + attn_rows
    share_out = jnp.concatenate(
        [
            lax.dynamic_slice_in_dim(mamba_out, mamba_rows * rep, mamba_rows, axis=0),
            lax.dynamic_slice_in_dim(attn_out, attn_rows * rep, attn_rows, axis=0),
        ],
        axis=0,
    )
    units = down_weight.shape[0] // reps
    if units % LANES:
        pick = lambda w: lax.dynamic_index_in_dim(
            w.reshape(depth, shards, reps, units), rep, axis=2, keepdims=False
        ).reshape(depth, shards * units)
        sources = (jnp.concatenate([pick(gate_weight), pick(up_weight)], axis=1),)
    else:
        sources = (gate_weight, up_weight)
    share_down = lax.dynamic_slice_in_dim(down_weight, units * rep, units, axis=0)

    live = (jnp.arange(length) < lengths[0]).astype(F32)[:, None]
    stream = tokens.astype(F32)
    live_wide = jnp.broadcast_to(live, (length, LANES))
    w_in, aux_all, branch_two, *made = gather_in_call(
        shards,
        cut,
        in_t,
        query_weight,
        key_weight,
        value_weight,
        aux,
        tokens,
        cotangent,
        live_wide,
    )
    if w_in.ndim == 3:
        w_in = jnp.moveaxis(w_in, 0, 1).reshape(cut.width, width)
    branch_two = branch_two.reshape(reps * length, width)
    share_out = lax.ppermute(share_out, ("fsdp", "rep"), pairs)

    put = lax.dynamic_update_slice
    inner_rows = mamba_rows * shards
    half_ff = shards * units

    aux_all = aux_all.reshape(shards, -1)[:, :aux_size].astype(F32)
    gain_one = aux_all[:, :depth].reshape(1, width)
    gain_two = aux_all[:, depth : 2 * depth].reshape(1, width)
    conv_all = aux_all[:, 2 * depth :].reshape(shards, CONV + 1, own)
    conv_all = conv_all.transpose(1, 0, 2).reshape(CONV + 1, channels)
    conv_own = jnp.concatenate(
        [columns(conv_all, cut.inner * rep, cut.inner), conv_all[:, INNER:]], axis=1
    )
    conv_own = jnp.pad(conv_own, ((0, 7 - CONV), (0, 0)))
    of_heads = lambda v: jnp.pad(
        lax.dynamic_slice_in_dim(v, cut.heads * rep, cut.heads), (0, LANES - cut.heads)
    )
    head_own = jnp.stack([of_heads(decay_log), of_heads(step_bias)])
    head_own = jnp.pad(head_own, ((0, 6), (0, 0)))
    chan_own = lax.dynamic_slice_in_dim(skip_gain, cut.heads * rep, cut.heads)
    chan_own = jnp.pad(jnp.repeat(chan_own, HDIM)[None, :], ((0, 7), (0, 0)))
    cosine, sine = turn_tables(length)

    if len(made) == 3:
        normed, proj, steps = made
    else:
        stream_all = made[0].reshape(reps * length, width).astype(F32)
        scale_all = norm_scale(stream_all)
        normed = low(stream_all * scale_all * gain_one)
        proj = dot_nt(normed, w_in)
        steps = proj[:, cut.step : cut.step + LANES]
        proj = low(proj)
    inside = depth % LANES == 0
    ordered = mamba_rows % 16 == 0 and attn_rows % 16 == 0
    w_out, w_down, mixed_heads = gather_rows_call(
        shards,
        cut,
        length,
        ordered,
        share_out,
        share_down,
        proj,
        steps,
        conv_own,
        head_own,
        chan_own,
        cosine,
        sine,
    )
    if not ordered:
        w_out = jnp.concatenate(
            [
                w_out[:, :mamba_rows].reshape(-1, width),
                w_out[:, mamba_rows:].reshape(-1, width),
            ],
            axis=0,
        )
    w_down = w_down.reshape(-1, width)
    gain_rows = jnp.broadcast_to(gain_two, (8, width))
    w_mlp, normed_two, mixed, *gate_up = gather_mlp_call(
        shards, inside, sources, 2 * half_ff, mixed_heads, w_out, tokens, live_wide, gain_rows
    )
    w_mlp = w_mlp.reshape(width, -1)
    normed_two = normed_two.reshape(reps * length, width)
    gate_up = gate_up[0] if inside else dot(normed_two, w_mlp)
    activated, d_gate_up, d_two = mlp_back_call(gate_up, branch_two, w_down, w_mlp)
    d_two = d_two.reshape(reps, length, width)
    branch_one, s_down, g_mlp, ffn, d_mixed, gain_two_sum = scatter_down_call(
        shards,
        d_two,
        branch_two,
        normed_two,
        d_gate_up,
        activated,
        w_down,
        mixed,
        cotangent,
        live_wide,
        gain_rows,
    )
    g_mlp = g_mlp.reshape(shards, depth, -1)
    ffn = ffn.reshape(reps, length, width)

    branch_one = branch_one.reshape(reps * length, width)
    d_heads = dot_nt(branch_one, w_out)
    g_out = low(dot_tn(mixed_heads, branch_one))
    if not ordered:
        g_out = jnp.concatenate(
            [
                g_out[:inner_rows].reshape(shards, mamba_rows, width),
                g_out[inner_rows:].reshape(shards, attn_rows, width),
            ],
            axis=1,
        )
    downs, came, s_mlp, s_out, d_proj, d_proj_t, conv_sum, head_sum, chan_sum = scatter_mlp_call(
        shards,
        cut,
        length,
        g_mlp,
        g_out,
        proj,
        steps,
        d_heads,
        conv_own,
        head_own,
        chan_own,
        cosine,
        sine,
        s_down,
        ffn,
    )
    ffn_sum = ffn[0].astype(F32) + came.astype(F32).sum(axis=0)
    output = low(mixed + live * ffn_sum)
    if inside:
        given = (d_proj_t, normed, d_proj, w_in)
        gain_one_sum = jnp.zeros((width,), F32)
    else:
        g_in = low(dot(d_proj_t, normed))
        g_in = jnp.moveaxis(g_in.reshape(2 * cut.way, shards, depth), 1, 0)
        d_one = dot(d_proj, w_in)
        gain_one_sum = jnp.sum(d_one * stream_all * scale_all, axis=0)
        given = (g_in, low(d_one).reshape(reps, length, width))

    conv_sums = jnp.zeros((CONV + 1, channels), F32)
    conv_sums = put(conv_sums, conv_sum[: CONV + 1, : cut.inner], (0, cut.inner * rep))
    conv_sums = put(conv_sums, conv_sum[: CONV + 1, cut.inner :], (0, INNER))
    head_sums = jnp.zeros((3, HEADS), F32)
    own_sums = jnp.stack(
        [
            head_sum[0, : cut.heads],
            head_sum[1, : cut.heads],
            jnp.sum(chan_sum[0].reshape(cut.heads, HDIM), axis=1),
        ]
    )
    head_sums = put(head_sums, own_sums, (0, cut.heads * rep))
    small = jnp.concatenate(
        [
            gain_one_sum.reshape(shards, depth),
            gain_two_sum[0].reshape(shards, depth),
            conv_sums.reshape(CONV + 1, shards, own).transpose(1, 0, 2).reshape(shards, -1),
            jnp.broadcast_to(head_sums.reshape(1, -1), (shards, 3 * HEADS)),
        ],
        axis=1,
    )
    small_size = small.shape[1]
    tall = 32
    small = jnp.pad(low(small), ((0, 0), (0, tall * LANES - small_size)))
    small = small.reshape(shards, tall, LANES)
    ins, smalls, mlps, outs, grad_tokens = scatter_in_call(
        shards,
        depth,
        inside,
        given,
        small,
        tokens,
        d_mixed,
        jnp.broadcast_to(gain_one, (8, width)),
        s_mlp,
        s_out,
    )

    places = jnp.stack([rep ^ member for member in rep_order(reps)]).astype(jnp.int32)
    spread = functools.partial(spread_call, places)
    out_mamba, out_attn = spread(
        outs,
        [(mamba_rows * reps, width), (attn_rows * reps, width)],
        [
            (0, slice(0, mamba_rows), slice(0, width), mamba_rows, 0, 0),
            (1, slice(mamba_rows, out_rows), slice(0, width), attn_rows, 0, 0),
        ],
    )
    (out_down,) = spread(
        downs,
        [(units * reps, width)],
        [(0, slice(0, units), slice(0, width), units, 0, 0)],
    )
    out_gate, out_up = spread(
        mlps,
        [(depth, half_ff * reps)] * 2,
        [
            (
                which,
                slice(0, depth),
                slice(which * half_ff + shard * units, which * half_ff + (shard + 1) * units),
                0,
                units,
                shard * units * reps,
            )
            for which in range(2)
            for shard in range(shards)
        ],
    )
    out_wide, out_query, out_key, out_value = spread_in_call(cut, places, ins)
    out_proj = out_wide.T
    small = smalls.astype(F32).sum(axis=0).reshape(-1)[:small_size]
    out_gain_one = small[:depth]
    out_gain_two = small[depth : 2 * depth]
    conv_sums = small[2 * depth : 2 * depth + (CONV + 1) * own].reshape(CONV + 1, own)
    out_decay, out_step, out_skip = small[2 * depth + (CONV + 1) * own :].reshape(3, HEADS)
    return (
        output,
        grad_tokens,
        out_gain_one,
        out_proj,
        conv_sums[:CONV],
        conv_sums[CONV],
        out_decay,
        out_step,
        out_skip,
        out_query,
        out_key,
        out_value,
        out_mamba,
        out_attn,
        out_gain_two,
        out_gate,
        out_up,
        out_down,
    )


def solution(mesh):
    rows = P(("fsdp", "rep"), None)
    shard = P("fsdp", None)
    in_specs = (
        rows,
        P(("fsdp", "rep")),
        P("fsdp"),
        shard,
        P(None, "fsdp"),
        P("fsdp"),
        P(),
        P(),
        P(),
        shard,
        shard,
        shard,
        shard,
        shard,
        P("fsdp"),
        shard,
        shard,
        shard,
        rows,
    )
    out_specs = (
        rows,
        rows,
        P("fsdp"),
        shard,
        P(None, "fsdp"),
        P("fsdp"),
        P(),
        P(),
        P(),
        shard,
        shard,
        shard,
        shard,
        shard,
        P("fsdp"),
        shard,
        shard,
        shard,
    )
    sizes = (mesh.shape["fsdp"], mesh.shape["rep"])
    return jax.shard_map(
        functools.partial(on_device, sizes),
        mesh=mesh,
        in_specs=in_specs,
        out_specs=out_specs,
        check_vma=False,
    )
```

time: 4670 us -> 752 us (0.16)
  waiting for transfers between devices: 3680 us -> 0.01 us
  Pallas kernels: 0 us -> 693 us
  matrix products: 354 us -> 16.3 us
  local copies, waits for them, and re-layouts: 285 us -> 21.4 us
  blocking collectives: 180 us -> 0 us
  other arithmetic: 105 us -> 5.69 us
    reduce_scatter x9 -> x0, waiting for transfers between devices: 2120 us -> none  [the longest x1 857 us: on_device(): lax.psum_scatter(grad_proj, 'fsdp', scatter_dimension=0, tiled=True)]
    all_gather x9 -> x0, waiting for transfers between devices: 1290 us -> none  [the longest x1 515 us: on_device(): lax.all_gather(in_proj, 'fsdp', axis=0, tiled=True)]
    pallas_call x0 -> x11, Pallas kernels: none -> 693 us  [the longest x1 136 us: scatter_in_call(): pl.pallas_call(functools.partial(scatter_in, shards, inside), out_shape=[...]
    dot_general x62 -> x2, matrix products: 354 us -> 16.3 us  [dot(): lax.dot_general(left, right, (contract, ((), ())), preferred_element_type...]
    psum x2 -> x0, waiting for transfers between devices: 258 us -> none  [the longest x1 218 us: on_device(): lax.psum((shard_gain_one, shard_proj, shard_conv, shard_bias, shard_query...]
    dynamic_update_slice x6 -> x3, local copies, waits for them, and re-layouts: 149 us -> 1.72 us  [the longest x1 0.75 us: on_device(): put(conv_sums, conv_sum[:CONV + 1, :cut.inner], (0, cut.inner * rep))]
    psum x3 -> x0, blocking collectives: 70.1 us -> none  [the longest x1 43 us: on_device(): lax.psum((decay_grad, step_grad, skip_grad), ('fsdp', 'rep'))]
    unnamed x3 -> x0, blocking collectives: 56.3 us -> none
  transfers between devices with their start and end apart: 21 -> 1, of which waited for: 16 -> 0; matrix products, arithmetic and copies ran while one was open for 15% -> 1% of each run, Pallas kernels for 0% -> 16%
where the time goes in v1:
time: 752 us; the launch traced here: 742 us
  Pallas kernels  693 us (92%)
  local copies, waits for them, and re-layouts  21.4 us (3%)
  matrix products  16.3 us (2%)
    pallas_call x1, Pallas kernels, scatter_in_call(): pl.pallas_call(functools.partial(scatter_in, shards, inside), out_shape=[...  136 us
    pallas_call x1, Pallas kernels, scatter_mlp_call(): pl.pallas_call(functools.partial(scatter_mlp, shards, cut, length), out_s...  135 us
    pallas_call x1, Pallas kernels, gather_in_call(): pl.pallas_call(functools.partial(gather_in, shards, cut, inside), out_sha...  121 us
    pallas_call x1, Pallas kernels, gather_mlp_call(): pl.pallas_call(functools.partial(gather_mlp, shards, inside, len(sources)...  98.8 us
    pallas_call x1, Pallas kernels, gather_rows_call(): pl.pallas_call(functools.partial(gather_rows, shards, cut, length), out_s...  93.7 us
    pallas_call x1, Pallas kernels, scatter_down_call(): pl.pallas_call(functools.partial(scatter_down, shards), out_shape=[jax.Sh...  70.1 us
    pallas_call x1, Pallas kernels, mlp_back_call(): pl.pallas_call(mlp_back, grid=(rows // tall,), out_shape=[jax.ShapeDtypeS...  22.8 us
    dot_general x2, matrix products, dot(): lax.dot_general(left, right, (contract, ((), ())), preferred_element_type...  16.3 us
  transfers between devices with their start and end apart: 1, of which 0 were waited for; matrix products, arithmetic and copies ran while one was open for 1% of the time, Pallas kernels for 16%

profile of v1, /device:TPU:11, one launch (start us, length us, event | category | flops | bytes accessed | tf_op | source)
XLA Modules:
  0.0 741.6 jit_solution(12774144136988905880)
XLA Ops:
  0.7 1.2 constant_dynamic-slice_fusion.3
  1.9 0.9 constant_dynamic-slice_fusion.2
  2.9 3.1 collective-permute-start
  6.7 0.8 reshape.133
  7.5 0.7 fusion.7
  8.2 0.6 reshape.134.refs_4_
  8.8 0.8 broadcast_in_dim.38.refs_7_.refs_5_.live_ref
  9.5 121.5 %gather_in.1 = (bf16[2688,2048]{1,0:T(8,128)(2,1)}, bf16[8,16,256]{2,1,0:T(8,128)(2,1)}, bf16[4,256,2048]{2,1,0:T(8,128)(2,1)}, bf16[1024,2048]{1,0:T(8,128)(2,1...) custom-call(bf16[6704,256]{1,0:T(8,128)(2,1)} %bitcast.54, bf16[256,1024]{1,0:T(8,128)(2,1)} %refs_1_.2, ...), custom_call_target="tpu_custom_call" | custom-call | tf_op jit(solution)/shard_map/gather_in/pallas_call | solution.py:802
  131.0 0.9 copy.39
  132.3 0.1 reshape.137
  132.7 0.5 fusion
  133.3 0.1 pad_maximum_fusion.1
  133.6 1.0 copy-done.5
  134.6 93.7 %gather_rows.1 = (bf16[1024,2048]{1,0:T(8,128)(2,1)}, bf16[8,128,2048]{2,1,0:T(8,128)(2,1)}, bf16[1024,1024]{1,0:T(8,128)(2,1)S(1)}) custom-call(bf16[128,2048]{1,0:T(8,128)(2,1)S(1)} %collective-permute-done.heads_ref, bf16[128,2048]{1,0:T(8,128)(2,1)S(1)} %constant_dynamic-slice_fusion.1.down_ref, bf16[1024,2688]{1,0:T(8,128)(2,1)} %get-tuple-element.62.proj_ref, ...), custom_call_target="tpu_custom_call" | custom-call | tf_op jit(solution)/shard_map/gather_rows/pallas_call | solution.py:913
  228.4 1.3 copy-done.7
  229.8 0.6 broadcast_in_dim.41.refs_6_.gain_ref
  230.4 98.8 %gather_mlp.1 = (bf16[8,256,2048]{2,1,0:T(8,128)(2,1)}, bf16[4,256,2048]{2,1,0:T(8,128)(2,1)}, f32[256,2048]{1,0:T(8,128)}, f32[1024,2048]{1,0:T(8,128)}) custom-call(bf16[256,4096]{1,0:T(8,128)(2,1)} %refs_0_.1, bf16[256,4096]{1,0:T(8,128)(2,1)} %refs_1_.3, bf16[1024,1024]{1,0:T(8,128)(2,1)} %copy-done.7, bf16[1024,2048]{1,0:T(8,128)(2,1)} %get-tuple-element.66.refs_3_, ...), custom_call_target="tpu_custom_call" | custom-call | tf_op jit(solution)/shard_map/gather_mlp/pallas_call | solution.py:1293
  329.2 22.8 %mlp_back.1 = (bf16[1024,1024]{1,0:T(8,128)(2,1)}, bf16[1024,2048]{1,0:T(8,128)(2,1)}, bf16[1024,2048]{1,0:T(8,128)(2,1)}) custom-call(f32[1024,2048]{1,0:T(8,128)} %get-tuple-element.68.gate_up_ref, bf16[1024,2048]{1,0:T(8,128)(2,1)} %bitcast.45, bf16[1024,2048]{1,0:T(8,128)(2,1)} %bitcast.47, bf16[2048,2048]{1,0:T(8,128)(2,1)} %bitcast.49), custom_call_target="tpu_custom_call" | custom-call | tf_op jit(solution)/shard_map/mlp_back/pallas_call | solution.py:1359
  352.0 70.1 %scatter_down.1 = (bf16[4,256,2048]{2,1,0:T(8,128)(2,1)}, bf16[128,2048]{1,0:T(8,128)(2,1)}, bf16[2048,2048]{1,0:T(8,128)(2,1)}, bf16[1024,2048]{1,0:T(8,128)(2,...) custom-call(bf16[4,256,2048]{2,1,0:T(8,128)(2,1)} %bitcast.53, bf16[1024,2048]{1,0:T(8,128)(2,1)} %bitcast.46, ...), custom_call_target="tpu_custom_call" | custom-call | tf_op jit(solution)/shard_map/scatter_down/pallas_call | solution.py:1484
  422.2 10.1 %fusion.10.grad_ref = f32[1024,1024]{1,0:T(8,128)} fusion(bf16[1024,2048]{1,0:T(8,128)(2,1)} %bitcast.66, bf16[1024,2048]{1,0:T(8,128)(2,1)} %get-tuple-element.66.refs_3_), kind=kOutput, calls=%fused_computation.46 | convolution fusion | flops 4294967296 | bytes 12582912 | tf_op jit(solution)/shard_map/dot_general | solution.py:30
  432.3 6.2 convolution_convert_fusion.out_ref
  438.5 135.0 %scatter_mlp.1 = (bf16[4,128,2048]{2,1,0:T(8,128)(2,1)}, bf16[3,256,2048]{2,1,0:T(8,128)(2,1)}, bf16[256,2048]{1,0:T(8,128)(2,1)}, bf16[128,2048]{1,0:T(8,128)(2...) custom-call(bf16[8,256,2048]{2,1,0:T(8,128)(2,1)} %bitcast.50, ...), custom_call_target="tpu_custom_call" | custom-call | tf_op jit(solution)/shard_map/scatter_mlp/pallas_call | solution.py:1682
  573.5 0.8 slice_reduce_fusion
  574.3 0.1 reduce_sum.28
  574.4 0.7 slice.85
  575.1 0.3 dynamic_update_slice.11
  575.5 0.7 slice_dynamic-update-slice_fusion
  576.2 0.7 slice_dynamic-update-slice_fusion.1
  577.0 0.1 reshape.147
  577.1 0.1 reshape.148
  577.2 0.9 fusion.8
  578.2 0.6 copy.44
  578.9 0.6 broadcast_in_dim.47.refs_7_
  579.5 135.6 %scatter_in.1 = (bf16[4,2304,256]{2,1,0:T(8,128)(2,1)}, bf16[4,32,128]{2,1,0:T(8,128)(2,1)}, bf16[4,256,2048]{2,1,0:T(8,128)(2,1)}, bf16[4,128,2048]{2,1,0:T(8,128)(2,1)}, bf16[256,2048]{1,0:T(8,128)(2,1)}) custom-call(bf16[2304,1024]{1,0:T(8,128)(2,1)} %get-tuple-element.81.refs_0_, bf16[1024,2048]{1,0:T(8,128)(2,1)} %get-tuple-element.82.refs_1_, ...), custom_call_target="tpu_custom_call" | custom-call | tf_op jit(solution)/shard_map/scatter_in/pallas_call | solution.py:1894
  715.1 0.8 convert_reduce_fusion.1
  715.9 0.6 slice_bitcast_fusion.2
  716.5 0.6 slice.103
  717.1 0.6 fusion.9
  717.6 2.3 copy-done.2
  720.0 4.9 spread_in.1
  724.9 5.1 spread.4
  729.9 2.8 spread.3
  732.7 0.7 slice.91
  733.4 2.8 spread.5
  736.3 0.6 convert_reduce_fusion
  736.9 0.9 copy-done.14
  737.8 2.6 add_convert_fusion
  740.5 1.0 copy.50
  (75 shorter events, 1.2 us)
Async XLA Ops:
  0.7 132.9 %copy-start = (bf16[512,2048]{1,0:T(8,128)(2,1)S(1)}, bf16[512,2048]{1,0:T(8,128)(2,1)}, u32[]{:S(2)}) copy-start(bf16[512,2048]{1,0:T(8,128)(2,1)} %param.36) | copy-start | bytes 6291460
  1.9 130.1 %copy-start.18 = (f32[48]{0:T(128)S(1)}, f32[48]{0:T(128)}, u32[]{:S(2)}) copy-start(f32[48]{0:T(128)} %param.25) | copy-start | bytes 580
  1.9 130.2 %copy-start.19 = (f32[48]{0:T(128)S(1)}, f32[48]{0:T(128)}, u32[]{:S(2)}) copy-start(f32[48]{0:T(128)} %param.26) | copy-start | bytes 580
  2.8 129.6 %copy-start.20 = (f32[48]{0:T(128)S(1)}, f32[48]{0:T(128)}, u32[]{:S(2)}) copy-start(f32[48]{0:T(128)} %param.27) | copy-start | bytes 580
  2.9 130.7 %collective-permute-start = (bf16[128,2048]{1,0:T(8,128)(2,1)S(1)}, bf16[128,2048]{1,0:T(8,128)(2,1)S(1)}, u32[]{:S(2)}, u32[]{:S(2)}) collective-permute-start(bf16[128,2048]{1,0:T(8,128)(2,1)S(1)} %pad_maximum_fusion), channel_id=1, source_target_pairs={{0,0},{1,4},{2,8},{3,12},{4,16},{5,20},{6,24},{7,28},{8,1},{9,5},{... | collective-permute-start | bytes 1572872 | tf_op jit(solution)/shard_map/ppermute | solution.py:2042
  132.7 95.7 %copy-start.13 = (f32[8,128]{1,0:T(8,128)}, f32[8,128]{1,0:T(8,128)S(1)}, u32[]{:S(2)}) copy-start(f32[8,128]{1,0:T(8,128)S(1)} %select_maximum_fusion.1.head_ref) | copy-start | bytes 12292
  132.7 95.7 %copy-start.12 = (f32[8,768]{1,0:T(8,128)}, f32[8,768]{1,0:T(8,128)S(1)}, u32[]{:S(2)}) copy-start(f32[8,768]{1,0:T(8,128)S(1)} %pad.32.chan_ref) | copy-start | bytes 73732
  133.4 95.0 %copy-start.9 = (f32[256,128]{1,0:T(8,128)}, f32[256,128]{1,0:T(8,128)S(1)}, u32[]{:S(2)}) copy-start(f32[256,128]{1,0:T(8,128)S(1)} %get-tuple-element.118.cos_ref) | copy-start | bytes 393220
  133.4 95.0 %copy-start.10 = (f32[256,128]{1,0:T(8,128)}, f32[256,128]{1,0:T(8,128)S(1)}, u32[]{:S(2)}) copy-start(f32[256,128]{1,0:T(8,128)S(1)} %get-tuple-element.119.sin_ref) | copy-start | bytes 393220
  133.5 94.9 %copy-start.11 = (f32[8,1280]{1,0:T(8,128)}, f32[8,1280]{1,0:T(8,128)S(1)}, u32[]{:S(2)}) copy-start(f32[8,1280]{1,0:T(8,128)S(1)} %select_maximum_fusion.conv_ref) | copy-start | bytes 122884
  133.6 1.0 copy-start.5
  228.4 1.3 copy-start.7
  422.1 10.2 %copy-start.8 = (bf16[1024,1024]{1,0:T(8,128)(2,1)S(1)}, bf16[1024,1024]{1,0:T(8,128)(2,1)}, u32[]{:S(2)}) copy-start(bf16[1024,1024]{1,0:T(8,128)(2,1)} %copy-done.7) | copy-start | bytes 6291460
  422.2 10.2 %copy-start.17 = (bf16[4,256,2048]{2,1,0:T(8,128)(2,1)S(1)}, bf16[4,256,2048]{2,1,0:T(8,128)(2,1)}, u32[]{:S(2)}) copy-start(bf16[4,256,2048]{2,1,0:T(8,128)(2,1)} %get-tuple-element.78) | copy-start | bytes 12582916
  717.6 2.3 copy-start.2
  720.0 4.9 copy-start.3
  720.0 10.0 %copy-start.6 = (bf16[4,128,2048]{2,1,0:T(8,128)(2,1)S(1)}, bf16[4,128,2048]{2,1,0:T(8,128)(2,1)}, u32[]{:S(2)}) copy-start(bf16[4,128,2048]{2,1,0:T(8,128)(2,1)} %get-tuple-element.99.blocks_ref) | copy-start | bytes 6291460
  724.9 8.6 %copy-start.4 = (bf16[4,128,2048]{2,1,0:T(8,128)(2,1)S(1)}, bf16[4,128,2048]{2,1,0:T(8,128)(2,1)}, u32[]{:S(2)}) copy-start(bf16[4,128,2048]{2,1,0:T(8,128)(2,1)} %get-tuple-element.105.blocks_ref) | copy-start | bytes 6291460
  733.4 2.8 copy-start.15
  736.3 1.6 copy-start.14
  736.3 5.2 copy-start.1
  737.8 2.6 copy-start.16

commit v2 on v1

--- a/solution.py
+++ b/solution.py
@@ -554,22 +554,14 @@
     return ref.at[index, rows]
 
 
-def gather_in(shards, cut, inside, *refs):
+def gather_in(shards, cut, *refs):
     refs = list(refs)
     take = lambda number: [refs.pop(0) for _ in range(number)]
     in_ref, query_ref, key_ref, value_ref, aux_ref, tokens_ref, cot_ref, live_ref = take(8)
-    w_ref, aux_all_ref, branch_all_ref = take(3)
-    if inside:
-        normed_ref, proj_ref, steps_ref = take(3)
-    else:
-        (tokens_all_ref,) = take(1)
+    w_ref, aux_all_ref, branch_all_ref, tokens_all_ref = take(4)
     share_ref, turn_ref, rows_ref, branch_ref = take(4)
     pack_sem, send, recv, core_send, core_recv = take(5)
     token_sems, branch_sems = take(3), take(3)
-    if inside:
-        sum_ref, scale_ref, w_sem, w_out_ref = take(4)
-        w_ref, w_out_ref = w_out_ref, w_ref
-        tokens_all_ref = take(1)[0]
 
     ring, pair = Ring(shards), Pair()
     rep, core = pair.rep, pair.rep % 2
@@ -668,85 +660,20 @@
     tokens.pass_on(0)
     gather.advance(4)
     branch.pass_on(0)
-    gather.advance(5)
+    gather.run(5, shards)
+    gather.finish()
     tokens.finish()
+    branch.finish()
     for keep in keeps:
         keep.wait()
-    if inside:
-        length = tokens_ref.shape[0]
-        chunk = cut.width // 7
-
-        def scale(number, carry):
-            values = tokens_all_ref[number].astype(F32)
-            rows = pl.ds(pl.multiple_of(number * length, length), length)
-            scale_ref[rows] = jnp.broadcast_to(norm_scale(values), (length, LANES))
-            return carry
-
-        lax.fori_loop(0, 4, scale, 0)
-
-    def add(offset, fresh=False, last=False):
-        index = ring.at(offset)
-        if not fresh:
-            over_core(offset, 1, 1 - core).wait_recv()
-            over_core(shards - offset, 0, 1 - core).wait_recv()
-        lanes = pl.ds(pl.multiple_of(index * depth, LANES), depth)
-        gain = aux_all_ref[index, 0:1, :].astype(F32)
-
-        def body(number, carry):
-            rows = pl.ds(pl.multiple_of(number * length, length), length)
-            left = tokens_all_ref[number, :, lanes].astype(F32) * scale_ref[rows, 0:1] * gain
-            left = left.astype(BF16)
-            normed_ref[rows, lanes] = left
-            for at in range(0, cut.width, chunk):
-                out = slice(at, at + chunk)
-                total = dot_nt(left, w_ref[out, lanes])
-                if not fresh:
-                    total = sum_ref[rows, out] + total
-                if not last:
-                    sum_ref[rows, out] = total
-                    continue
-                proj_ref[rows, out] = total.astype(BF16)
-                if at <= cut.step < at + chunk:
-                    steps_ref[rows] = total[:, cut.step - at : cut.step - at + LANES]
-            return carry
-
-        lax.fori_loop(0, 4, body, 0)
-        store(offset).start()
-
-    def store(offset):
-        lanes = pl.ds(pl.multiple_of(ring.at(offset) * depth, LANES), depth)
-        return pltpu.make_async_copy(w_ref.at[:, lanes], w_out_ref.at[:, lanes], w_sem.at[offset])
-
-    done = {0}
-    if inside:
-        add(0, True)
-
-    def add_landed(step):
-        for offset in range(1, shards):
-            if inside and offset not in done and max(offset, shards - offset) <= step:
-                done.add(offset)
-                add(offset, False, len(done) == shards)
-
-    add_landed(4)
-    gather.advance(6)
-    add_landed(5)
-    gather.run(7, shards)
-    add_landed(shards - 2)
-    gather.finish()
-    add_landed(shards - 1)
 
     def rest(step, carry):
         for way in range(2):
-            if not inside:
-                over_core(step, way, 1 - core).wait_recv()
+            over_core(step, way, 1 - core).wait_recv()
             over_core(step, way, core).wait_send()
         return carry
 
     lax.fori_loop(1, shards, rest, 0)
-    branch.finish()
-    if inside:
-        for offset in range(shards):
-            store(offset).wait()
 
 
 def share_sems(chunks):
@@ -760,7 +687,6 @@
 def gather_in_call(shards, cut, in_t, query, key, value, aux, tokens, cot, live):
     depth = in_t.shape[1]
     length, width = tokens.shape
-    inside = depth % LANES == 0
     hbm = pl.BlockSpec(memory_space=pl.ANY)
     vmem = pl.BlockSpec(memory_space=pltpu.VMEM)
     out_shape = [
@@ -779,34 +705,22 @@
         *share_sems(1),
         *share_sems(1),
     ]
-    if inside:
-        rows = 4 * length
-        out_shape = [jax.ShapeDtypeStruct((cut.width, width), BF16)] + out_shape
-        out_shape += [
-            jax.ShapeDtypeStruct((rows, width), BF16),
-            jax.ShapeDtypeStruct((rows, cut.width), BF16),
-            jax.ShapeDtypeStruct((rows, LANES), F32),
-        ]
-        out_specs = [hbm, vmem, hbm] + [vmem] * 3
-        scratch += [
-            pltpu.VMEM((rows, cut.width), F32),
-            pltpu.VMEM((rows, LANES), F32),
-            pltpu.SemaphoreType.DMA((shards,)),
-            pltpu.VMEM((cut.width, width), BF16),
-            pltpu.VMEM((4, length, width), BF16),
-        ]
+    if depth % LANES:
+        w_shape = (shards, cut.width, depth)
     else:
-        out_shape = [jax.ShapeDtypeStruct((shards, cut.width, depth), BF16)] + out_shape
-        out_shape += [jax.ShapeDtypeStruct((4, length, width), BF16)]
-        out_specs = [hbm] * 4
+        w_shape = (cut.width, width)
     return pl.pallas_call(
-        functools.partial(gather_in, shards, cut, inside),
-        out_shape=out_shape,
+        functools.partial(gather_in, shards, cut),
+        out_shape=[
+            jax.ShapeDtypeStruct(w_shape, BF16),
+            *out_shape,
+            jax.ShapeDtypeStruct((4, length, width), BF16),
+        ],
         in_specs=[hbm] * 6 + [vmem] * 2,
-        out_specs=out_specs,
+        out_specs=[hbm] * 4,
         scratch_shapes=scratch,
         compiler_params=pltpu.CompilerParams(
-            collective_id=0, has_side_effects=True, vmem_limit_bytes=56 * MIB
+            collective_id=0, has_side_effects=True, vmem_limit_bytes=40 * MIB
         ),
         name="gather_in",
     )(in_t, query, key, value, aux, tokens, cot, live)
@@ -818,8 +732,9 @@
     length,
     heads_ref,
     down_ref,
-    proj_ref,
-    step_ref,
+    w_ref,
+    tokens_ref,
+    gain_ref,
     conv_ref,
     head_ref,
     chan_ref,
@@ -828,6 +743,9 @@
     heads_all_ref,
     down_all_ref,
     out_ref,
+    normed_ref,
+    proj_ref,
+    step_ref,
     act_ref,
     pack_sem,
     send,
@@ -878,6 +796,27 @@
     gather = Gather(ring, ways, send, recv)
     gather.start()
     count = proj_ref.shape[0] // length
+    wide = cut.width // 7
+
+    def norm(number, carry):
+        rows = pl.ds(pl.multiple_of(number * length, length), length)
+        values = tokens_ref[number].astype(F32)
+        normed_ref[rows] = (values * norm_scale(values) * gain_ref[0:1]).astype(BF16)
+        return carry
+
+    def project(tile, carry):
+        out = pl.ds(pl.multiple_of(tile * wide, LANES), wide)
+        proj_ref[:, out] = dot_nt(normed_ref[...], w_ref[out]).astype(BF16)
+        return carry
+
+    lax.fori_loop(0, count, norm, 0)
+    first = dot_nt(normed_ref[...], w_ref[:wide])
+    proj_ref[:, :wide] = first.astype(BF16)
+    step_ref[...] = first[:, cut.step : cut.step + LANES]
+    lax.fori_loop(1, 4, project, 0)
+    gather.advance(2)
+    lax.fori_loop(4, 7, project, 0)
+    gather.advance(3)
 
     def body(number, carry):
         rows = pl.ds(pl.multiple_of(number * length, length), length)
@@ -893,20 +832,20 @@
             out_ref.at[rows],
             act_ref,
         )
-        gather.advance(number + 2)
+        gather.advance(number + 4)
         return carry
 
     lax.fori_loop(0, count, body, 0)
-    gather.run(count + 2, shards)
+    gather.run(count + 4, shards)
     gather.finish()
     for pack in packs:
         pack.wait()
 
 
 def gather_rows_call(
-    shards, cut, length, ordered, heads, down, proj, steps, conv, head, chan, cosine, sine
+    shards, cut, length, ordered, heads, down, w, tokens, gain, conv, head, chan, cosine, sine
 ):
-    rows = proj.shape[0]
+    rows = 4 * length
     tall, width = heads.shape
     hbm = pl.BlockSpec(memory_space=pl.ANY)
     vmem = pl.BlockSpec(memory_space=pltpu.VMEM)
@@ -918,9 +857,12 @@
             ),
             jax.ShapeDtypeStruct((shards,) + down.shape, BF16),
             jax.ShapeDtypeStruct((rows, cut.inner + cut.qwidth), BF16),
+            jax.ShapeDtypeStruct((rows, width), BF16),
+            jax.ShapeDtypeStruct((rows, cut.width), BF16),
+            jax.ShapeDtypeStruct((rows, LANES), F32),
         ],
-        in_specs=[vmem] * 9,
-        out_specs=[hbm] * 2 + [vmem],
+        in_specs=[vmem] * 10,
+        out_specs=[hbm] * 2 + [vmem] * 4,
         scratch_shapes=[
             pltpu.VMEM((length, cut.conv), F32),
             pltpu.SemaphoreType.DMA((4,)),
@@ -930,7 +872,7 @@
             collective_id=1, has_side_effects=True, vmem_limit_bytes=48 * MIB
         ),
         name="gather_rows",
-    )(heads, down, proj, steps, conv, head, chan, cosine, sine)
+    )(heads, down, w, tokens, gain, conv, head, chan, cosine, sine)
 
 
 class Exchange:
@@ -1056,7 +998,10 @@
 
 
 class Scatter:
-    def __init__(self, ring, pieces, term, first_ref, slots_ref, send, recv, groups=1):
+    def __init__(
+        self, ring, pieces, term, first_ref, slots_ref, send, recv, groups=1, made_ref=None
+    ):
+        self.made = made_ref
         self.ring, self.pieces, self.groups, self.term = ring, pieces, groups, term
         self.first, self.slots, self.send, self.recv = first_ref, slots_ref, send, recv
         self.half = slots_ref.shape[2]
@@ -1075,6 +1020,9 @@
         return pl.ds(piece * self.tall, self.tall)
 
     def due(self, step, way, piece):
+        if self.made is not None:
+            at = piece % (self.pieces // self.groups) * self.tall
+            return self.made[way, at : at + self.tall]
         return self.term(self.ring.at((2 * way - 1) * step), self.rows(way, piece))
 
     def copy(self, step, way, piece, first=False):
@@ -1097,7 +1045,16 @@
             self.ring.peer(way),
         )
 
+    def make(self, step, group):
+        if self.made is None:
+            return
+        tall = self.half // self.groups
+        for way in range(2):
+            index = self.ring.at((2 * way - 1) * step)
+            self.made[way] = self.term(index, pl.ds(way * self.half + group * tall, tall))
+
     def start(self, group=0):
+        self.make(1, group)
         for way, piece in self.each(group):
             self.first[way, self.local(piece)] = self.due(1, way, piece).astype(BF16)
             self.copy(1, way, piece, True).start()
@@ -1108,6 +1065,7 @@
         return self.slots[step - 2, way, self.local(piece)].astype(F32) + term
 
     def advance(self, step, group=0):
+        self.make(step, group)
         for way, piece in self.each(group):
             total = self.total(step, way, piece)
             self.slots[step - 2, way, self.local(piece)] = total.astype(BF16)
@@ -1121,6 +1079,7 @@
         lax.fori_loop(first, stop, body, 0)
 
     def result(self, own_ref, share=None, group=0):
+        self.make(self.ring.shards, group)
         for way, piece in self.each(group):
             total = self.total(self.ring.shards, way, piece)
             own_ref[self.rows(way, piece)] = total.astype(BF16)
@@ -1229,21 +1188,28 @@
         own_ref[rows] = (mixed * norm_scale(mixed) * gain_ref[0:1]).astype(BF16)
         share.start(chunk)
 
-    def add(index, fresh=False):
+    def add(offsets, fresh=False):
         if not inside:
             return
-        deep = pl.ds(pl.multiple_of(index * depth, LANES), depth)
-
-        def body(number, carry):
-            left = normed_ref[number, :, deep]
-            rows = pl.ds(pl.multiple_of(number * length, length), length)
-            for lane in range(0, wide, WIDE):
-                lanes = slice(lane, lane + WIDE)
-                term = dot(left, all_ref[index, :, lanes])
-                sum_ref[rows, lanes] = term if fresh else sum_ref[rows, lanes] + term
+        blocks = [ring.at(offset) for offset in offsets]
+
+        def body(tile, carry):
+            lanes = pl.ds(pl.multiple_of(tile * WIDE, LANES), WIDE)
+            left = jnp.concatenate(
+                [
+                    normed_ref[
+                        :, :, pl.ds(pl.multiple_of(index * depth, LANES), depth)
+                    ].reshape(4 * length, depth)
+                    for index in blocks
+                ],
+                axis=1,
+            )
+            right = jnp.concatenate([all_ref[index, :, lanes] for index in blocks], axis=0)
+            term = dot(left, right)
+            sum_ref[:, lanes] = term if fresh else sum_ref[:, lanes] + term
             return carry
 
-        lax.fori_loop(0, 4, body, 0)
+        lax.fori_loop(0, wide // WIDE, body, 0)
 
     gather.start()
     for number in (3, 2, 1, 0):
@@ -1264,23 +1230,20 @@
     share.finish()
     keep.wait()
     half_way = shards // 2
-    add(ring.index, True)
     if half_way < 6:
-        add(ring.at(half_way))
+        add((0, half_way), True)
     gather.run(7, shards)
     if half_way >= 6:
-        add(ring.at(half_way))
+        add((0, half_way), True)
     if inside:
 
         def body(far, carry):
-            add(ring.at(far))
-            add(ring.at(-far))
+            add((far, -far))
             return carry
 
         lax.fori_loop(2, half_way, body, 0)
     gather.finish()
-    add(ring.at(1))
-    add(ring.at(-1))
+    add((1, -1))
     exchange.finish()
 
 
@@ -1736,7 +1699,7 @@
     mlp_sems, out_sems = take(3), take(3)
     move_ref, move_sem = take(2)
     if inside:
-        d_ref, w_ref, part_ref, small_all, gain_sum_ref, load_sem = take(6)
+        d_ref, w_ref, part_ref, small_all, gain_sum_ref, load_sem, made_ref = take(7)
 
     ring, pair = Ring(shards), Pair()
     if inside:
@@ -1776,7 +1739,14 @@
         stay.start()
 
     pieces = PIECES
-    scatter = Scatter(ring, pieces, term, *in_scratch, groups=GROUPS)
+    scatter = Scatter(
+        ring,
+        pieces,
+        term,
+        *in_scratch,
+        groups=GROUPS,
+        made_ref=made_ref if inside else None,
+    )
     small = Scatter(ring, 1, small_term, *small_scratch)
     exchange = Exchange(
         pair, CHUNKS, part_ref, core_ref, cross_ref, came_ref, (ex_send, ex_recv)
@@ -1793,21 +1763,17 @@
         d_values, _ = norm_back(values, norm_scale(values), gain_ref[0:1], grad)
         grad_ref[rows] = (d_mixed_ref[rows] + d_values).astype(BF16)
 
-    def partial(number):
+    def partial(tile):
         length = part_ref.shape[1]
-        wide = 4 * LANES
-        rows = pl.ds(number * length, length)
-
-        def body(tile, carry):
-            lanes = pl.ds(pl.multiple_of(tile * wide, wide), wide)
-            grad = dot(d_ref[rows], w_ref[:, lanes])
-            part_ref[number, :, lanes] = grad.astype(BF16)
-            gain_sum_ref[0:1, lanes] += jnp.sum(
-                grad * normed_ref[rows, lanes].astype(F32), axis=0, keepdims=True
-            )
-            return carry
-
-        lax.fori_loop(0, w_ref.shape[1] // wide, body, 0)
+        wide = part_ref.shape[2] // 4
+        lanes = slice(tile * wide, (tile + 1) * wide)
+        grad = dot(d_ref[...], w_ref[:, lanes])
+        for number in range(4):
+            rows = slice(number * length, (number + 1) * length)
+            part_ref[number, :, lanes] = grad[rows].astype(BF16)
+        gain_sum_ref[0:1, lanes] = jnp.sum(
+            grad * normed_ref[:, lanes].astype(F32), axis=0, keepdims=True
+        )
 
     scatter.start(0)
     for chunk in range(CHUNKS):
@@ -1890,6 +1856,7 @@
             pltpu.VMEM(small.shape, BF16),
             pltpu.VMEM((8, width), F32),
             pltpu.SemaphoreType.DMA((2,)),
+            pltpu.VMEM((2, wide // (2 * GROUPS), depth), F32),
         ]
     return pl.pallas_call(
         functools.partial(scatter_in, shards, inside),
@@ -2024,7 +1991,7 @@
     live = (jnp.arange(length) < lengths[0]).astype(F32)[:, None]
     stream = tokens.astype(F32)
     live_wide = jnp.broadcast_to(live, (length, LANES))
-    w_in, aux_all, branch_two, *made = gather_in_call(
+    w_in, aux_all, branch_two, tokens_all = gather_in_call(
         shards,
         cut,
         in_t,
@@ -2063,26 +2030,18 @@
     chan_own = jnp.pad(jnp.repeat(chan_own, HDIM)[None, :], ((0, 7), (0, 0)))
     cosine, sine = turn_tables(length)
 
-    if len(made) == 3:
-        normed, proj, steps = made
-    else:
-        stream_all = made[0].reshape(reps * length, width).astype(F32)
-        scale_all = norm_scale(stream_all)
-        normed = low(stream_all * scale_all * gain_one)
-        proj = dot_nt(normed, w_in)
-        steps = proj[:, cut.step : cut.step + LANES]
-        proj = low(proj)
     inside = depth % LANES == 0
     ordered = mamba_rows % 16 == 0 and attn_rows % 16 == 0
-    w_out, w_down, mixed_heads = gather_rows_call(
+    w_out, w_down, mixed_heads, normed, proj, steps = gather_rows_call(
         shards,
         cut,
         length,
         ordered,
         share_out,
         share_down,
-        proj,
-        steps,
+        w_in,
+        tokens_all,
+        jnp.broadcast_to(gain_one, (8, width)),
         conv_own,
         head_own,
         chan_own,
@@ -2160,6 +2119,8 @@
         g_in = low(dot(d_proj_t, normed))
         g_in = jnp.moveaxis(g_in.reshape(2 * cut.way, shards, depth), 1, 0)
         d_one = dot(d_proj, w_in)
+        stream_all = tokens_all.reshape(reps * length, width).astype(F32)
+        scale_all = norm_scale(stream_all)
         gain_one_sum = jnp.sum(d_one * stream_all * scale_all, axis=0)
         given = (g_in, low(d_one).reshape(reps, length, width))
 

time: 752 us -> 753 us (level)
    pallas_call x1, Pallas kernels: 121 us -> 107 us  [gather_in_call(): pl.pallas_call(functools.partial(gather_in, shards, cut), out_shape=[jax....]
    pallas_call x1, Pallas kernels: 70.1 us -> 80.7 us  [scatter_down_call(): pl.pallas_call(functools.partial(scatter_down, shards), out_shape=[jax.Sh...]
    unnamed x49 -> x67, local copies, waits for them, and re-layouts: 8.22 us -> 16.5 us
  transfers between devices with their start and end apart: 1 -> 1, of which waited for: 0 -> 0; matrix products, arithmetic and copies ran while one was open for 1% -> 0% of each run, Pallas kernels for 16% -> 14%
where the time goes in v2:
time: 753 us; the launch traced here: 749 us
  Pallas kernels  694 us (92%)
  local copies, waits for them, and re-layouts  27.7 us (4%)
  matrix products  16.3 us (2%)
    pallas_call x1, Pallas kernels, scatter_in_call(): pl.pallas_call(functools.partial(scatter_in, shards, inside), out_shape=[...  136 us
    pallas_call x1, Pallas kernels, scatter_mlp_call(): pl.pallas_call(functools.partial(scatter_mlp, shards, cut, length), out_s...  134 us
    pallas_call x1, Pallas kernels, gather_in_call(): pl.pallas_call(functools.partial(gather_in, shards, cut), out_shape=[jax....  107 us
    pallas_call x1, Pallas kernels, gather_rows_call(): pl.pallas_call(functools.partial(gather_rows, shards, cut, length), out_s...  100 us
    pallas_call x1, Pallas kernels, gather_mlp_call(): pl.pallas_call(functools.partial(gather_mlp, shards, inside, len(sources)...  98.9 us
    pallas_call x1, Pallas kernels, scatter_down_call(): pl.pallas_call(functools.partial(scatter_down, shards), out_shape=[jax.Sh...  80.7 us
    pallas_call x1, Pallas kernels, mlp_back_call(): pl.pallas_call(mlp_back, grid=(rows // tall,), out_shape=[jax.ShapeDtypeS...  22.7 us
    unnamed x67, local copies, waits for them, and re-layouts  16.5 us
  transfers between devices with their start and end apart: 1, of which 0 were waited for; matrix products, arithmetic and copies ran while one was open for 0% of the time, Pallas kernels for 14%

profile of v2, /device:TPU:11, one launch (start us, length us, event | category | flops | bytes accessed | tf_op | source)
XLA Modules:
  0.0 749.4 jit_solution(17511007309751663889)
XLA Ops:
  0.7 1.2 constant_dynamic-slice_fusion.3
  1.9 0.9 constant_dynamic-slice_fusion.2
  2.9 3.1 collective-permute-start
  6.7 0.8 reshape.133
  7.4 0.7 fusion.7
  8.3 1.3 copy-done.3
  9.5 1.2 copy-done.5
  10.8 2.0 copy-done.7
  12.7 1.0 copy-done.16
  13.8 0.9 copy-done.20
  14.7 0.9 copy-done.21
  15.6 106.8 %gather_in.1 = (bf16[2688,2048]{1,0:T(8,128)(2,1)}, bf16[8,16,256]{2,1,0:T(8,128)(2,1)S(1)}, bf16[4,256,2048]{2,1,0:T(8,128)(2,1)S(1)}, bf16[4,256,2048]{2,1,0:T(8,128)(2,1)}) custom-call(bf16[6704,256]{1,0:T(8,128)(2,1)S(1)} %bitcast.47, bf16[256,1024]{1,0:T(8,128)(2,1)S(1)} %copy-done.16, bf16[256,256]{1,0:T(8,128)(2,1)S(1)} %copy-done.20, ...), custom_call_target="tpu_custom_call" | custom-call | tf_op jit(solution)/shard_map/gather_in/pallas_call | solution.py:712
  122.4 2.0 copy-done.2
  125.2 0.5 fusion
  125.8 0.1 pad_maximum_fusion.1
  126.2 100.1 %gather_rows.1 = (bf16[1024,2048]{1,0:T(8,128)(2,1)}, bf16[8,128,2048]{2,1,0:T(8,128)(2,1)}, bf16[1024,1024]{1,0:T(8,128)(2,1)S(1)}, bf16[1024,2048]{1,0:T(8,128...) custom-call(bf16[128,2048]{1,0:T(8,128)(2,1)S(1)} %collective-permute-done.heads_ref, ...), custom_call_target="tpu_custom_call" | custom-call | tf_op jit(solution)/shard_map/gather_rows/pallas_call | solution.py:852
  226.3 1.3 copy-done.11
  227.6 0.8 copy-done.17
  228.4 0.6 broadcast_in_dim.46.refs_6_.gain_ref
  229.1 98.9 %gather_mlp.1 = (bf16[8,256,2048]{2,1,0:T(8,128)(2,1)}, bf16[4,256,2048]{2,1,0:T(8,128)(2,1)}, f32[256,2048]{1,0:T(8,128)}, f32[1024,2048]{1,0:T(8,128)}) custom-call(bf16[256,4096]{1,0:T(8,128)(2,1)} %refs_0_.1, bf16[256,4096]{1,0:T(8,128)(2,1)} %refs_1_.3, bf16[1024,1024]{1,0:T(8,128)(2,1)} %copy-done.11, bf16[1024,2048]{1,0:T(8,128)(2,1)} %get-tuple-element.67.refs_3_, ...), custom_call_target="tpu_custom_call" | custom-call | tf_op jit(solution)/shard_map/gather_mlp/pallas_call | solution.py:1256
  327.9 22.7 %mlp_back.1 = (bf16[1024,1024]{1,0:T(8,128)(2,1)}, bf16[1024,2048]{1,0:T(8,128)(2,1)}, bf16[1024,2048]{1,0:T(8,128)(2,1)}) custom-call(f32[1024,2048]{1,0:T(8,128)} %get-tuple-element.69.gate_up_ref, bf16[1024,2048]{1,0:T(8,128)(2,1)} %bitcast.45, bf16[1024,2048]{1,0:T(8,128)(2,1)} %bitcast.49, bf16[2048,2048]{1,0:T(8,128)(2,1)} %bitcast.51), custom_call_target="tpu_custom_call" | custom-call | tf_op jit(solution)/shard_map/mlp_back/pallas_call | solution.py:1322
  350.6 80.7 %scatter_down.1 = (bf16[4,256,2048]{2,1,0:T(8,128)(2,1)}, bf16[128,2048]{1,0:T(8,128)(2,1)}, bf16[2048,2048]{1,0:T(8,128)(2,1)}, bf16[1024,2048]{1,0:T(8,128)(2,...) custom-call(bf16[4,256,2048]{2,1,0:T(8,128)(2,1)} %bitcast.55, bf16[1024,2048]{1,0:T(8,128)(2,1)} %bitcast.46, ...), custom_call_target="tpu_custom_call" | custom-call | tf_op jit(solution)/shard_map/scatter_down/pallas_call | solution.py:1447
  431.3 10.1 %fusion.10.grad_ref = f32[1024,1024]{1,0:T(8,128)} fusion(bf16[1024,2048]{1,0:T(8,128)(2,1)} %bitcast.66, bf16[1024,2048]{1,0:T(8,128)(2,1)} %get-tuple-element.67.refs_3_), kind=kOutput, calls=%fused_computation.46 | convolution fusion | flops 4294967296 | bytes 12582912 | tf_op jit(solution)/shard_map/dot_general | solution.py:30
  441.4 6.2 convolution_convert_fusion.out_ref
  447.6 134.0 %scatter_mlp.1 = (bf16[4,128,2048]{2,1,0:T(8,128)(2,1)}, bf16[3,256,2048]{2,1,0:T(8,128)(2,1)}, bf16[256,2048]{1,0:T(8,128)(2,1)}, bf16[128,2048]{1,0:T(8,128)(2...) custom-call(bf16[8,256,2048]{2,1,0:T(8,128)(2,1)} %bitcast.52, ...), custom_call_target="tpu_custom_call" | custom-call | tf_op jit(solution)/shard_map/scatter_mlp/pallas_call | solution.py:1645
  581.7 0.8 slice_reduce_fusion
  582.5 0.1 reduce_sum.28
  582.6 0.7 slice.86
  583.3 0.3 dynamic_update_slice.11
  583.7 0.7 slice_dynamic-update-slice_fusion
  584.4 0.7 slice_dynamic-update-slice_fusion.1
  585.4 0.9 fusion.8
  586.4 0.6 copy.44
  587.0 135.8 %scatter_in.1 = (bf16[4,2304,256]{2,1,0:T(8,128)(2,1)}, bf16[4,32,128]{2,1,0:T(8,128)(2,1)}, bf16[4,256,2048]{2,1,0:T(8,128)(2,1)}, bf16[4,128,2048]{2,1,0:T(8,128)(2,1)}, bf16[256,2048]{1,0:T(8,128)(2,1)}) custom-call(bf16[2304,1024]{1,0:T(8,128)(2,1)} %get-tuple-element.84.refs_0_, bf16[1024,2048]{1,0:T(8,128)(2,1)} %get-tuple-element.85.refs_1_, ...), custom_call_target="tpu_custom_call" | custom-call | tf_op jit(solution)/shard_map/scatter_in/pallas_call | solution.py:1861
  722.8 0.8 convert_reduce_fusion.1
  723.6 0.6 slice_bitcast_fusion.2
  724.2 0.6 slice.103
  724.7 0.6 fusion.9
  725.3 2.3 copy-done.4
  727.7 4.9 spread_in.1
  732.6 5.1 spread.4
  737.6 2.8 spread.3
  740.4 0.7 slice.91
  741.1 2.8 spread.5
  744.0 0.6 convert_reduce_fusion
  744.6 0.9 copy-done.23
  745.5 2.6 add_convert_fusion
  748.2 1.0 copy.50
  (93 shorter events, 1.7 us)
Async XLA Ops:
  0.7 125.4 %copy-start = (bf16[512,2048]{1,0:T(8,128)(2,1)S(1)}, bf16[512,2048]{1,0:T(8,128)(2,1)}, u32[]{:S(2)}) copy-start(bf16[512,2048]{1,0:T(8,128)(2,1)} %param.36) | copy-start | bytes 6291460
  1.9 122.6 %copy-start.27 = (f32[48]{0:T(128)S(1)}, f32[48]{0:T(128)}, u32[]{:S(2)}) copy-start(f32[48]{0:T(128)} %param.25) | copy-start | bytes 580
  1.9 122.7 %copy-start.28 = (f32[48]{0:T(128)S(1)}, f32[48]{0:T(128)}, u32[]{:S(2)}) copy-start(f32[48]{0:T(128)} %param.26) | copy-start | bytes 580
  2.8 122.1 %copy-start.29 = (f32[48]{0:T(128)S(1)}, f32[48]{0:T(128)}, u32[]{:S(2)}) copy-start(f32[48]{0:T(128)} %param.27) | copy-start | bytes 580
  2.9 123.3 %collective-permute-start = (bf16[128,2048]{1,0:T(8,128)(2,1)S(1)}, bf16[128,2048]{1,0:T(8,128)(2,1)S(1)}, u32[]{:S(2)}, u32[]{:S(2)}) collective-permute-start(bf16[128,2048]{1,0:T(8,128)(2,1)S(1)} %pad_maximum_fusion), channel_id=1, source_target_pairs={{0,0},{1,4},{2,8},{3,12},{4,16},{5,20},{6,24},{7,28},{8,1},{9,5},{... | collective-permute-start | bytes 1572872 | tf_op jit(solution)/shard_map/ppermute | solution.py:2009
  8.2 117.7 %copy-start.8 = (f32[256,128]{1,0:T(8,128)}, f32[256,128]{1,0:T(8,128)S(1)}, u32[]{:S(2)}) copy-start(f32[256,128]{1,0:T(8,128)S(1)} %broadcast_in_dim.20.refs_7_.refs_5_.live_ref) | copy-start | bytes 393220
  8.3 1.3 copy-start.3
  9.5 1.2 copy-start.5
  10.8 2.0 copy-start.7
  12.7 1.0 copy-start.16
  13.8 0.9 copy-start.20
  14.7 0.9 copy-start.21
  122.4 2.0 copy-start.2
  125.2 101.1 %copy-start.22 = (f32[8,128]{1,0:T(8,128)}, f32[8,128]{1,0:T(8,128)S(1)}, u32[]{:S(2)}) copy-start(f32[8,128]{1,0:T(8,128)S(1)} %select_maximum_fusion.1.head_ref) | copy-start | bytes 12292
  125.2 101.0 %copy-start.19 = (f32[8,768]{1,0:T(8,128)}, f32[8,768]{1,0:T(8,128)S(1)}, u32[]{:S(2)}) copy-start(f32[8,768]{1,0:T(8,128)S(1)} %pad.32.chan_ref) | copy-start | bytes 73732
  125.9 100.3 %copy-start.13 = (f32[256,128]{1,0:T(8,128)}, f32[256,128]{1,0:T(8,128)S(1)}, u32[]{:S(2)}) copy-start(f32[256,128]{1,0:T(8,128)S(1)} %get-tuple-element.120.cos_ref) | copy-start | bytes 393220
  125.9 100.3 %copy-start.14 = (f32[256,128]{1,0:T(8,128)}, f32[256,128]{1,0:T(8,128)S(1)}, u32[]{:S(2)}) copy-start(f32[256,128]{1,0:T(8,128)S(1)} %get-tuple-element.121.sin_ref) | copy-start | bytes 393220
  126.1 100.2 %copy-start.18 = (f32[8,1280]{1,0:T(8,128)}, f32[8,1280]{1,0:T(8,128)S(1)}, u32[]{:S(2)}) copy-start(f32[8,1280]{1,0:T(8,128)S(1)} %select_maximum_fusion.conv_ref) | copy-start | bytes 122884
  126.2 100.2 %copy-start.15 = (f32[8,2048]{1,0:T(8,128)}, f32[8,2048]{1,0:T(8,128)S(1)}, u32[]{:S(2)}) copy-start(f32[8,2048]{1,0:T(8,128)S(1)} %broadcast_in_dim.43.gain_ref.refs_7_) | copy-start | bytes 196612
  226.3 1.3 copy-start.11
  227.6 0.8 copy-start.17
  431.3 10.2 %copy-start.12 = (bf16[1024,1024]{1,0:T(8,128)(2,1)S(1)}, bf16[1024,1024]{1,0:T(8,128)(2,1)}, u32[]{:S(2)}) copy-start(bf16[1024,1024]{1,0:T(8,128)(2,1)} %copy-done.11) | copy-start | bytes 6291460
  431.3 10.2 %copy-start.26 = (bf16[4,256,2048]{2,1,0:T(8,128)(2,1)S(1)}, bf16[4,256,2048]{2,1,0:T(8,128)(2,1)}, u32[]{:S(2)}) copy-start(bf16[4,256,2048]{2,1,0:T(8,128)(2,1)} %get-tuple-element.79) | copy-start | bytes 12582916
  725.3 2.3 copy-start.4
  727.7 4.9 copy-start.6
  727.7 10.0 %copy-start.10 = (bf16[4,128,2048]{2,1,0:T(8,128)(2,1)S(1)}, bf16[4,128,2048]{2,1,0:T(8,128)(2,1)}, u32[]{:S(2)}) copy-start(bf16[4,128,2048]{2,1,0:T(8,128)(2,1)} %get-tuple-element.101.blocks_ref) | copy-start | bytes 6291460
  732.5 8.6 %copy-start.9 = (bf16[4,128,2048]{2,1,0:T(8,128)(2,1)S(1)}, bf16[4,128,2048]{2,1,0:T(8,128)(2,1)}, u32[]{:S(2)}) copy-start(bf16[4,128,2048]{2,1,0:T(8,128)(2,1)} %get-tuple-element.107.blocks_ref) | copy-start | bytes 6291460
  741.1 2.8 copy-start.24
  743.9 1.6 copy-start.23
  743.9 5.2 copy-start.1
  745.5 2.6 copy-start.25

commit v3 on v2

--- a/solution.py
+++ b/solution.py
@@ -630,12 +630,12 @@
 
     ways = (
         [
+            piece(shared(core, 0)),
             piece(rows(0)),
             piece(rows(1)),
-            piece(shared(core, 0)),
             (aux_ref, lambda index: aux_all_ref.at[index]),
         ],
-        [piece(rows(2)), piece(rows(3)), piece(shared(core, 1))],
+        [piece(shared(core, 1)), piece(rows(2)), piece(rows(3))],
     )
 
     def over_core(step, way, which):
@@ -645,7 +645,7 @@
         )
 
     def hook(step, way, piece):
-        if piece == 2:
+        if piece == 0:
             over_core(step, way, core).start()
 
     gather = Gather(ring, ways, send, recv, hook)

time: 753 us -> 752 us (level)
  no operation moved by 1% of the time
where the time goes in v3:
time: 752 us; the launch traced here: 748 us
  Pallas kernels  693 us (92%)
  local copies, waits for them, and re-layouts  27.7 us (4%)
  matrix products  16.3 us (2%)
    pallas_call x1, Pallas kernels, scatter_in_call(): pl.pallas_call(functools.partial(scatter_in, shards, inside), out_shape=[...  136 us
    pallas_call x1, Pallas kernels, scatter_mlp_call(): pl.pallas_call(functools.partial(scatter_mlp, shards, cut, length), out_s...  135 us
    pallas_call x1, Pallas kernels, gather_in_call(): pl.pallas_call(functools.partial(gather_in, shards, cut), out_shape=[jax....  105 us
    pallas_call x1, Pallas kernels, gather_rows_call(): pl.pallas_call(functools.partial(gather_rows, shards, cut, length), out_s...  99.9 us
    pallas_call x1, Pallas kernels, gather_mlp_call(): pl.pallas_call(functools.partial(gather_mlp, shards, inside, len(sources)...  98.2 us
    pallas_call x1, Pallas kernels, scatter_down_call(): pl.pallas_call(functools.partial(scatter_down, shards), out_shape=[jax.Sh...  80.5 us
    pallas_call x1, Pallas kernels, mlp_back_call(): pl.pallas_call(mlp_back, grid=(rows // tall,), out_shape=[jax.ShapeDtypeS...  22.7 us
    unnamed x67, local copies, waits for them, and re-layouts  16.5 us
  transfers between devices with their start and end apart: 1, of which 0 were waited for; matrix products, arithmetic and copies ran while one was open for 0% of the time, Pallas kernels for 14%

profile of v3, /device:TPU:11, one launch (start us, length us, event | category | flops | bytes accessed | tf_op | source)
XLA Modules:
  0.0 748.3 jit_solution(4167271122989309414)
XLA Ops:
  0.7 1.2 constant_dynamic-slice_fusion.3
  1.9 0.9 constant_dynamic-slice_fusion.2
  2.9 3.1 collective-permute-start
  6.7 0.8 reshape.133
  7.4 0.7 fusion.7
  8.3 1.3 copy-done.3
  9.5 1.2 copy-done.5
  10.8 2.0 copy-done.7
  12.7 1.0 copy-done.16
  13.8 0.9 copy-done.20
  14.7 0.9 copy-done.21
  15.6 105.4 %gather_in.1 = (bf16[2688,2048]{1,0:T(8,128)(2,1)}, bf16[8,16,256]{2,1,0:T(8,128)(2,1)S(1)}, bf16[4,256,2048]{2,1,0:T(8,128)(2,1)S(1)}, bf16[4,256,2048]{2,1,0:T(8,128)(2,1)}) custom-call(bf16[6704,256]{1,0:T(8,128)(2,1)S(1)} %bitcast.47, bf16[256,1024]{1,0:T(8,128)(2,1)S(1)} %copy-done.16, bf16[256,256]{1,0:T(8,128)(2,1)S(1)} %copy-done.20, ...), custom_call_target="tpu_custom_call" | custom-call | tf_op jit(solution)/shard_map/gather_in/pallas_call | solution.py:712
  121.0 2.0 copy-done.2
  123.9 0.5 fusion
  124.4 0.1 pad_maximum_fusion.1
  124.8 99.9 %gather_rows.1 = (bf16[1024,2048]{1,0:T(8,128)(2,1)}, bf16[8,128,2048]{2,1,0:T(8,128)(2,1)}, bf16[1024,1024]{1,0:T(8,128)(2,1)S(1)}, bf16[1024,2048]{1,0:T(8,128...) custom-call(bf16[128,2048]{1,0:T(8,128)(2,1)S(1)} %collective-permute-done.heads_ref, ...), custom_call_target="tpu_custom_call" | custom-call | tf_op jit(solution)/shard_map/gather_rows/pallas_call | solution.py:852
  224.7 1.3 copy-done.11
  226.1 0.8 copy-done.17
  226.8 0.6 broadcast_in_dim.46.refs_6_.gain_ref
  227.5 98.2 %gather_mlp.1 = (bf16[8,256,2048]{2,1,0:T(8,128)(2,1)}, bf16[4,256,2048]{2,1,0:T(8,128)(2,1)}, f32[256,2048]{1,0:T(8,128)}, f32[1024,2048]{1,0:T(8,128)}) custom-call(bf16[256,4096]{1,0:T(8,128)(2,1)} %refs_0_.1, bf16[256,4096]{1,0:T(8,128)(2,1)} %refs_1_.3, bf16[1024,1024]{1,0:T(8,128)(2,1)} %copy-done.11, bf16[1024,2048]{1,0:T(8,128)(2,1)} %get-tuple-element.67.refs_3_, ...), custom_call_target="tpu_custom_call" | custom-call | tf_op jit(solution)/shard_map/gather_mlp/pallas_call | solution.py:1256
  325.7 22.7 %mlp_back.1 = (bf16[1024,1024]{1,0:T(8,128)(2,1)}, bf16[1024,2048]{1,0:T(8,128)(2,1)}, bf16[1024,2048]{1,0:T(8,128)(2,1)}) custom-call(f32[1024,2048]{1,0:T(8,128)} %get-tuple-element.69.gate_up_ref, bf16[1024,2048]{1,0:T(8,128)(2,1)} %bitcast.45, bf16[1024,2048]{1,0:T(8,128)(2,1)} %bitcast.49, bf16[2048,2048]{1,0:T(8,128)(2,1)} %bitcast.51), custom_call_target="tpu_custom_call" | custom-call | tf_op jit(solution)/shard_map/mlp_back/pallas_call | solution.py:1322
  348.4 80.5 %scatter_down.1 = (bf16[4,256,2048]{2,1,0:T(8,128)(2,1)}, bf16[128,2048]{1,0:T(8,128)(2,1)}, bf16[2048,2048]{1,0:T(8,128)(2,1)}, bf16[1024,2048]{1,0:T(8,128)(2,...) custom-call(bf16[4,256,2048]{2,1,0:T(8,128)(2,1)} %bitcast.55, bf16[1024,2048]{1,0:T(8,128)(2,1)} %bitcast.46, ...), custom_call_target="tpu_custom_call" | custom-call | tf_op jit(solution)/shard_map/scatter_down/pallas_call | solution.py:1447
  429.0 10.1 %fusion.10.grad_ref = f32[1024,1024]{1,0:T(8,128)} fusion(bf16[1024,2048]{1,0:T(8,128)(2,1)} %bitcast.66, bf16[1024,2048]{1,0:T(8,128)(2,1)} %get-tuple-element.67.refs_3_), kind=kOutput, calls=%fused_computation.46 | convolution fusion | flops 4294967296 | bytes 12582912 | tf_op jit(solution)/shard_map/dot_general | solution.py:30
  439.1 6.2 convolution_convert_fusion.out_ref
  445.3 134.9 %scatter_mlp.1 = (bf16[4,128,2048]{2,1,0:T(8,128)(2,1)}, bf16[3,256,2048]{2,1,0:T(8,128)(2,1)}, bf16[256,2048]{1,0:T(8,128)(2,1)}, bf16[128,2048]{1,0:T(8,128)(2...) custom-call(bf16[8,256,2048]{2,1,0:T(8,128)(2,1)} %bitcast.52, ...), custom_call_target="tpu_custom_call" | custom-call | tf_op jit(solution)/shard_map/scatter_mlp/pallas_call | solution.py:1645
  580.2 0.8 slice_reduce_fusion
  581.0 0.1 reduce_sum.28
  581.2 0.7 slice.86
  581.9 0.3 dynamic_update_slice.11
  582.2 0.7 slice_dynamic-update-slice_fusion
  583.0 0.7 slice_dynamic-update-slice_fusion.1
  583.9 0.9 fusion.8
  585.0 0.6 copy.44
  585.6 136.2 %scatter_in.1 = (bf16[4,2304,256]{2,1,0:T(8,128)(2,1)}, bf16[4,32,128]{2,1,0:T(8,128)(2,1)}, bf16[4,256,2048]{2,1,0:T(8,128)(2,1)}, bf16[4,128,2048]{2,1,0:T(8,128)(2,1)}, bf16[256,2048]{1,0:T(8,128)(2,1)}) custom-call(bf16[2304,1024]{1,0:T(8,128)(2,1)} %get-tuple-element.84.refs_0_, bf16[1024,2048]{1,0:T(8,128)(2,1)} %get-tuple-element.85.refs_1_, ...), custom_call_target="tpu_custom_call" | custom-call | tf_op jit(solution)/shard_map/scatter_in/pallas_call | solution.py:1861
  721.8 0.8 convert_reduce_fusion.1
  722.5 0.6 slice_bitcast_fusion.2
  723.1 0.6 slice.103
  723.7 0.6 fusion.9
  724.3 2.3 copy-done.4
  726.6 4.9 spread_in.1
  731.5 5.1 spread.4
  736.6 2.8 spread.3
  739.4 0.7 slice.91
  740.1 2.8 spread.5
  742.9 0.6 convert_reduce_fusion
  743.5 0.9 copy-done.23
  744.5 2.6 add_convert_fusion
  747.1 1.0 copy.50
  (93 shorter events, 1.7 us)
Async XLA Ops:
  0.7 124.0 %copy-start = (bf16[512,2048]{1,0:T(8,128)(2,1)S(1)}, bf16[512,2048]{1,0:T(8,128)(2,1)}, u32[]{:S(2)}) copy-start(bf16[512,2048]{1,0:T(8,128)(2,1)} %param.36) | copy-start | bytes 6291460
  1.9 121.3 %copy-start.27 = (f32[48]{0:T(128)S(1)}, f32[48]{0:T(128)}, u32[]{:S(2)}) copy-start(f32[48]{0:T(128)} %param.25) | copy-start | bytes 580
  1.9 121.3 %copy-start.28 = (f32[48]{0:T(128)S(1)}, f32[48]{0:T(128)}, u32[]{:S(2)}) copy-start(f32[48]{0:T(128)} %param.26) | copy-start | bytes 580
  2.8 120.7 %copy-start.29 = (f32[48]{0:T(128)S(1)}, f32[48]{0:T(128)}, u32[]{:S(2)}) copy-start(f32[48]{0:T(128)} %param.27) | copy-start | bytes 580
  2.9 121.9 %collective-permute-start = (bf16[128,2048]{1,0:T(8,128)(2,1)S(1)}, bf16[128,2048]{1,0:T(8,128)(2,1)S(1)}, u32[]{:S(2)}, u32[]{:S(2)}) collective-permute-start(bf16[128,2048]{1,0:T(8,128)(2,1)S(1)} %pad_maximum_fusion), channel_id=1, source_target_pairs={{0,0},{1,4},{2,8},{3,12},{4,16},{5,20},{6,24},{7,28},{8,1},{9,5},{... | collective-permute-start | bytes 1572872 | tf_op jit(solution)/shard_map/ppermute | solution.py:2009
  8.2 116.3 %copy-start.8 = (f32[256,128]{1,0:T(8,128)}, f32[256,128]{1,0:T(8,128)S(1)}, u32[]{:S(2)}) copy-start(f32[256,128]{1,0:T(8,128)S(1)} %broadcast_in_dim.20.refs_7_.refs_5_.live_ref) | copy-start | bytes 393220
  8.3 1.3 copy-start.3
  9.5 1.2 copy-start.5
  10.8 2.0 copy-start.7
  12.7 1.0 copy-start.16
  13.8 0.9 copy-start.20
  14.7 0.9 copy-start.21
  121.0 2.0 copy-start.2
  123.8 100.8 %copy-start.22 = (f32[8,128]{1,0:T(8,128)}, f32[8,128]{1,0:T(8,128)S(1)}, u32[]{:S(2)}) copy-start(f32[8,128]{1,0:T(8,128)S(1)} %select_maximum_fusion.1.head_ref) | copy-start | bytes 12292
  123.9 100.8 %copy-start.19 = (f32[8,768]{1,0:T(8,128)}, f32[8,768]{1,0:T(8,128)S(1)}, u32[]{:S(2)}) copy-start(f32[8,768]{1,0:T(8,128)S(1)} %pad.32.chan_ref) | copy-start | bytes 73732
  124.6 100.1 %copy-start.13 = (f32[256,128]{1,0:T(8,128)}, f32[256,128]{1,0:T(8,128)S(1)}, u32[]{:S(2)}) copy-start(f32[256,128]{1,0:T(8,128)S(1)} %get-tuple-element.120.cos_ref) | copy-start | bytes 393220
  124.6 100.1 %copy-start.14 = (f32[256,128]{1,0:T(8,128)}, f32[256,128]{1,0:T(8,128)S(1)}, u32[]{:S(2)}) copy-start(f32[256,128]{1,0:T(8,128)S(1)} %get-tuple-element.121.sin_ref) | copy-start | bytes 393220
  124.7 100.0 %copy-start.18 = (f32[8,1280]{1,0:T(8,128)}, f32[8,1280]{1,0:T(8,128)S(1)}, u32[]{:S(2)}) copy-start(f32[8,1280]{1,0:T(8,128)S(1)} %select_maximum_fusion.conv_ref) | copy-start | bytes 122884
  124.8 99.9 %copy-start.15 = (f32[8,2048]{1,0:T(8,128)}, f32[8,2048]{1,0:T(8,128)S(1)}, u32[]{:S(2)}) copy-start(f32[8,2048]{1,0:T(8,128)S(1)} %broadcast_in_dim.43.gain_ref.refs_7_) | copy-start | bytes 196612
  224.7 1.3 copy-start.11
  226.1 0.8 copy-start.17
  428.9 10.2 %copy-start.12 = (bf16[1024,1024]{1,0:T(8,128)(2,1)S(1)}, bf16[1024,1024]{1,0:T(8,128)(2,1)}, u32[]{:S(2)}) copy-start(bf16[1024,1024]{1,0:T(8,128)(2,1)} %copy-done.11) | copy-start | bytes 6291460
  428.9 10.2 %copy-start.26 = (bf16[4,256,2048]{2,1,0:T(8,128)(2,1)S(1)}, bf16[4,256,2048]{2,1,0:T(8,128)(2,1)}, u32[]{:S(2)}) copy-start(bf16[4,256,2048]{2,1,0:T(8,128)(2,1)} %get-tuple-element.79) | copy-start | bytes 12582916
  724.3 2.3 copy-start.4
  726.6 4.9 copy-start.6
  726.6 10.0 %copy-start.10 = (bf16[4,128,2048]{2,1,0:T(8,128)(2,1)S(1)}, bf16[4,128,2048]{2,1,0:T(8,128)(2,1)}, u32[]{:S(2)}) copy-start(bf16[4,128,2048]{2,1,0:T(8,128)(2,1)} %get-tuple-element.101.blocks_ref) | copy-start | bytes 6291460
  731.5 8.6 %copy-start.9 = (bf16[4,128,2048]{2,1,0:T(8,128)(2,1)S(1)}, bf16[4,128,2048]{2,1,0:T(8,128)(2,1)}, u32[]{:S(2)}) copy-start(bf16[4,128,2048]{2,1,0:T(8,128)(2,1)} %get-tuple-element.107.blocks_ref) | copy-start | bytes 6291460
  740.1 2.8 copy-start.24
  742.9 1.6 copy-start.23
  742.9 5.2 copy-start.1
  744.5 2.6 copy-start.25
